TPU v7x, 32 devices: a whole 2x2x4 slice. The times are simulated.
32 devices in a mesh: row: 4 (over y, core), col: 8 (over z, x).
Axes of the slice: x: 2, y: 2, z: 4, core: 2. Of those that a mesh axis runs over, the one named last changes fastest.
Arguments:
- observed: bfloat16 [64, 256, 188], P('row', 'col'), may hold values from -6 to 6
- library: bfloat16 [188, 2048], replicated, may hold values from -0.125 to 0.125
- warm: bfloat16 [64, 256, 2048], P('row', 'col'), may hold values from 0 to 1
- match_peer: int32 [16, 8, 8], P('row', 'col'), may hold values from 0 to 7
- match_slot: int32 [16, 8, 8], P('row', 'col'), may hold values from 0 to 1
- match_count: int32 [16, 8], P('row', 'col'), may hold values from 1 to 8
- match_weight: float32 [16, 8, 8], P('row', 'col'), may hold values from 0.1 to 10
- wanted: int32 [4, 64, 2], P('row', 'col'), may hold values from 0 to 3
- threshold: float32 [2048], replicated, may hold values from 0.02 to 0.2
Outputs:
- abundance: bfloat16 [64, 256, 2048], P('row', 'col')
- misfit: float32 [64, 256, 188], P('row', 'col')
Inputs may be any that keep to these rules, and one draw needn't show every extreme that they name: `match_peer`: col index along the device's own col group. `wanted`: every device names exactly 2 blocks, repeats allowed, of every device of its col group, itself included.
All inputs are finite; a program needn't handle non-finite values.
Results may differ from a plain program's by a relative error of at most 0.0025.
The roundings to bfloat16 on the way count: a program that leaves them out, or rounds other values in their place, can miss the bound.
Values may be sent and summed in bfloat16 or wider, within the bound.
A program may use at most 192 MiB of HBM per device.

v0:
```python
import jax
import jax.numpy as jnp
from jax import lax
from jax.sharding import PartitionSpec as P

BLOCK_ROWS = 4
ITERS = 2


MU = 1.0
GAMMA = 0.6
ETA = 0.3


def padded(block, sides, width):
    for axis, dim in sides:
        count = lax.axis_size(axis)
        forward = [(i, i + 1) for i in range(count - 1)]
        backward = [(target, source) for source, target in forward]
        low = lax.ppermute(
            lax.slice_in_dim(block, block.shape[dim] - width, None, axis=dim), axis, forward
        )
        high = lax.ppermute(lax.slice_in_dim(block, 0, width, axis=dim), axis, backward)
        block = jnp.concatenate([low, block, high], axis=dim)
    return block


def coefficients(peer, slot, count, weight, group, slots):
    ranks = jnp.arange(weight.shape[1], dtype=jnp.int32)
    live = ranks[None, :] < count[:, None]
    masked = jnp.where(live, weight, 0.0)
    share = masked / jnp.sum(masked, axis=1, keepdims=True)
    column = peer * slots + slot
    targets = jnp.arange(group * slots, dtype=jnp.int32)
    onehot = column[:, :, None] == targets[None, None, :]
    return jnp.sum(jnp.where(onehot, share[:, :, None], 0.0), axis=1).astype(jnp.bfloat16)


def solve_step(base, tile, dual, library, chol):
    right = base + MU * (tile.astype(jnp.float32) + dual)
    small = jnp.dot(right.astype(jnp.bfloat16), library.T, preferred_element_type=jnp.float32)
    solved = jax.scipy.linalg.cho_solve((chol, True), small.T)
    back = jnp.dot(solved.T.astype(jnp.bfloat16), library, preferred_element_type=jnp.float32)
    return (right - back) / MU


def neighbours(beside_all):
    total = (
        beside_all[:-2, 1:-1] + beside_all[2:, 1:-1] + beside_all[1:-1, :-2] + beside_all[1:-1, 2:]
    )
    return 0.25 * total


def update(primal, dual, averaged, spatial, threshold):
    blend = (primal - dual + GAMMA * averaged + ETA * spatial) / (1.0 + GAMMA + ETA)
    fresh = jnp.maximum(blend - threshold[None, :], 0.0)
    return (fresh.astype(jnp.bfloat16), dual - primal + fresh)


def local(
    observed, library, warm, match_peer, match_slot, match_count, match_weight, wanted, threshold
):
    tile_rows, tile_cols, atoms = warm.shape
    pixels = tile_rows * tile_cols
    blocks = tile_rows // BLOCK_ROWS
    block_pixels = BLOCK_ROWS * tile_cols
    group = lax.axis_size("col")
    slots = wanted.shape[2]
    gram = jnp.dot(library, library.T, preferred_element_type=jnp.float32) + MU * jnp.eye(
        library.shape[0], dtype=jnp.float32
    )
    chol = jnp.linalg.cholesky(gram)
    coef = coefficients(
        match_peer[:, 0], match_slot[:, 0], match_count[:, 0], match_weight[:, 0], group, slots
    )
    base = jnp.dot(observed.reshape(pixels, -1), library, preferred_element_type=jnp.float32)
    all_coefs = lax.all_gather(coef, "col", axis=0, tiled=True).reshape(
        group, blocks, group * slots
    )
    all_asked = lax.all_gather(wanted, "col", axis=0, tiled=True)
    offsets = jnp.arange(group, dtype=jnp.int32) * blocks
    picks = (all_asked + offsets[None, :, None]).reshape(group, group * slots)
    dual = jnp.zeros((pixels, atoms), jnp.float32)
    current = warm
    for step in range(ITERS):
        tiles = current.reshape(blocks, block_pixels, atoms)
        strip = lax.all_to_all(tiles, "col", split_axis=2, concat_axis=0, tiled=True)
        chosen = strip[picks].reshape(group, group * slots, -1)
        sums = jnp.einsum("cbj,cjx->cbx", all_coefs, chosen, preferred_element_type=jnp.float32)
        sums = sums.reshape(group * blocks, strip.shape[1], strip.shape[2])
        averaged = lax.all_to_all(sums, "col", split_axis=0, concat_axis=2, tiled=True)
        beside_all = padded(current, (("row", 0), ("col", 1)), 1).astype(jnp.float32)
        primal = solve_step(base, current.reshape(pixels, atoms), dual, library, chol)
        spatial = neighbours(beside_all).reshape(pixels, atoms)
        fresh, dual = update(primal, dual, averaged.reshape(pixels, atoms), spatial, threshold)
        current = fresh.reshape(tile_rows, tile_cols, atoms)
    rebuilt = jnp.dot(current.reshape(pixels, atoms), library.T, preferred_element_type=jnp.float32)
    misfit = observed.astype(jnp.float32) - rebuilt.reshape(tile_rows, tile_cols, -1)
    return (current, misfit)


def solution(mesh):
    return jax.shard_map(
        local,
        mesh=mesh,
        in_specs=(
            P("row", "col", None),
            P(),
            P("row", "col", None),
            P("row", "col", None),
            P("row", "col", None),
            P("row", "col"),
            P("row", "col", None),
            P("row", "col", None),
            P(),
        ),
        out_specs=(P("row", "col", None), P("row", "col", None)),
        check_vma=False,
    )
```

profile of v0, /device:TPU:17, one launch (start us, length us, event | category | flops | bytes accessed | tf_op | source)
XLA Modules:
  0.0 454.9 jit_solution(13374309105218437615)
XLA Ops:
  0.7 4.3 copy.101
  5.0 5.6 %all-to-all-start = ((bf16[4,128,2048]{1,0,2:T(4,128)(2,1)}), bf16[4,128,2048]{1,0,2:T(4,128)(2,1)S(1)}, u32[]{:S(2)}, u32[]{:S(2)}) async-start(bf16[4,128,2048]{1,0,2:T(4,128)(2,1)} %copy.101), calls=%async_computation | async-start | bytes 4194304 | tf_op jit(solution)/shard_map/all_to_all | solution.py:87
  10.6 52.3 %all_gather.7 = s32[8,8,2]{1,2,0:T(2,128)S(1)} all-gather(s32[1,8,2]{1,2,0:T(2,128)S(1)} %copy-done.22), channel_id=1, replica_groups=mesh['row'=4,'col'=8] {'col'}, dimensions={0}, use_global_device_ids=true | all-gather | bytes 576 | tf_op jit(solution)/shard_map/all_gather | solution.py:80
  63.5 10.8 %all-gather = bf16[8,4,16]{2,1,0:T(4,128)(2,1)S(1)} all-gather(bf16[1,4,16]{2,1,0:T(4,128)(2,1)S(1)} %bitcast.145), channel_id=1, replica_groups=mesh['row'=4,'col'=8] {'col'}, dimensions={0}, use_global_device_ids=true | all-gather | bytes 1152 | tf_op jit(solution)/shard_map/all_gather | solution.py:77
  78.8 6.5 %gather_fusion = bf16[128,128,256]{2,1,0:T(8,128)(2,1)} fusion(bf16[32,128,256]{2,1,0:T(8,128)(2,1)S(1)} %bitcast.126, s32[1024]{0:T(1024)S(1)} %pad_clamp_fusion), kind=kCustom, calls=%fused_computation | custom fusion | bytes 16777728 | tf_op jit(solution)/shard_map/gather | solution.py:88
  85.3 13.5 %reshape.179 = bf16[8,16,32768]{2,1,0:T(8,128)(2,1)} reshape(bf16[128,128,256]{2,1,0:T(8,128)(2,1)} %gather_fusion) | data formatting | bytes 16777216 | tf_op jit(solution)/shard_map/reshape | solution.py:88
  98.8 6.7 %fusion.52 = f32[8,4,32768]{2,1,0:T(4,128)} fusion(bf16[8,4,16]{2,1,0:T(4,128)(2,1)S(1)} %all-gather, bf16[8,16,32768]{2,1,0:T(8,128)(2,1)} %reshape.179), kind=kOutput, calls=%fused_computation.111 | convolution fusion | flops 33554432 | bytes 12583936 | tf_op jit(solution)/shard_map/cbj,cjx->cbx/dot_general | solution.py:89
  105.6 6.0 %reshape.180 = f32[32,128,256]{2,1,0:T(8,128)} reshape(f32[8,4,32768]{2,1,0:T(4,128)} %fusion.52) | data formatting | bytes 8388608 | tf_op jit(solution)/shard_map/reshape | solution.py:90
  111.6 10.5 %all-to-all-start.1 = ((f32[32,128,256]{2,1,0:T(8,128)}), f32[32,128,256]{2,1,0:T(8,128)}, u32[]{:S(2)}, u32[]{:S(2)}) async-start(f32[32,128,256]{2,1,0:T(8,128)} %reshape.180), calls=%async_computation.1 | async-start | bytes 8388608 | tf_op jit(solution)/shard_map/all_to_all | solution.py:91
  122.8 10.3 %collective-permute-start = (bf16[1,32,2048]{2,1,0:T(8,128)(2,1)}, bf16[1,32,2048]{2,1,0:T(8,128)(2,1)}, u32[]{:S(2)}, u32[]{:S(2)}) collective-permute-start(bf16[1,32,2048]{2,1,0:T(8,128)(2,1)} %get-tuple-element.37), channel_id=1, source_target_pairs={{0,8},{8,16},{16,24},{1,9},{9,17},{17,25},{2,10},{10,18},{18,26},{... | collective-permute-start | bytes 393224 | tf_op jit(solution)/shard_map/ppermute | solution.py:20
  139.2 11.7 %cholesky.51 = f32[128,128]{1,0:T(8,128)S(1)} custom-call(f32[128,128]{1,0:T(8,128)S(1)} %cholesky.124), custom_call_target="Cholesky" | custom-call | tf_op jit(solution)/shard_map/jit(cholesky)/cholesky | solution.py:72
  151.0 9.8 %custom-call.16 = f32[1,128,128]{1,2,0:T(8,128)S(1)} custom-call(f32[1,128,128]{2,1,0:T(8,128)S(1)} %get-tuple-element.40), custom_call_target="InvertDiagBlocksLowerTriangular" | custom-call | tf_op jit(solution)/shard_map/jit(cholesky)/cholesky | solution.py:72
  162.7 5.5 %cholesky.110 = f32[60,60]{1,0:T(8,128)S(1)} custom-call(f32[60,60]{1,0:T(8,128)S(1)} %convolution_subtract_fusion.5), custom_call_target="Cholesky" | custom-call | tf_op jit(solution)/shard_map/jit(cholesky)/cholesky | solution.py:72
  171.7 21.0 %custom-call.18 = f32[2,128,128]{1,2,0:T(8,128)S(1)} custom-call(f32[2,128,128]{2,1,0:T(8,128)} %pad_maximum_fusion), custom_call_target="InvertDiagBlocksLowerTriangular" | custom-call | tf_op jit(solution)/shard_map/jit(_cho_solve)/triangular_solve | solution.py:42
  199.7 3.1 collective-permute-start.2
  206.9 9.8 %collective-permute-done.2 = bf16[18,1,2048]{2,0,1:T(8,128)(2,1)S(1)} collective-permute-done((bf16[18,1,2048]{2,0,1:T(8,128)(2,1)S(1)}, bf16[18,1,2048]{2,0,1:T(8,128)(2,1)S(1)}, u32[]{:S(2)}, u32[]{:S(2)}) %collective-permute-start.2) | collective-permute-done | bytes 73760 | tf_op jit(solution)/shard_map/ppermute | solution.py:20
  220.9 4.4 copy.111
  233.2 5.0 %fusion.47 = (bf16[512,2048]{1,0:T(8,128)(2,1)S(1)}, f32[512,2048]{1,0:T(8,128)}, f32[512,2048]{1,0:T(8,128)}) fusion(f32[2048]{0:T(1024)S(1)} %copy-done.17, f32[16,32,2048]{2,1,0:T(8,128)S(1)} %copy-done.10, f32[512,2048]{1,0:T(8,128)S(1)} %bitcast.135, bf16[188,2048]{1,0:T(8,128)(2,1)S(1)} %copy-done, f32[60,512]{1,0:T(8,128)S(1)} %fusion.35, ...), kind=kOutput, calls=%fused_computation.107 | convolution fusion | flops 404086784 | bytes 26198016 | tf_op jit(solution)/shard_map/dot_general | solution.py:43
  240.8 50.8 %all_to_all.54 = bf16[4,128,2048]{1,0,2:T(4,128)(2,1)S(1)} all-to-all(bf16[4,128,2048]{1,0,2:T(4,128)(2,1)} %copy.112), channel_id=1, replica_groups=mesh['row'=4,'col'=8] {'col'}, dimensions={2} | all-to-all | bytes 4194304 | tf_op jit(solution)/shard_map/all_to_all | solution.py:87
  293.2 4.0 copy.114
  297.2 8.1 %gather_fusion.1 = bf16[128,128,256]{2,1,0:T(8,128)(2,1)} fusion(bf16[32,128,256]{2,1,0:T(8,128)(2,1)} %bitcast.125, s32[1024]{0:T(1024)S(1)} %pad_clamp_fusion), kind=kCustom, calls=%fused_computation.1 | custom fusion | bytes 16777728 | tf_op jit(solution)/shard_map/gather | solution.py:88
  305.3 13.5 %reshape.181 = bf16[8,16,32768]{2,1,0:T(8,128)(2,1)} reshape(bf16[128,128,256]{2,1,0:T(8,128)(2,1)} %gather_fusion.1) | data formatting | bytes 16777216 | tf_op jit(solution)/shard_map/reshape | solution.py:88
  318.8 6.7 %fusion.53 = f32[8,4,32768]{2,1,0:T(4,128)} fusion(bf16[8,4,16]{2,1,0:T(4,128)(2,1)S(1)} %all-gather, bf16[8,16,32768]{2,1,0:T(8,128)(2,1)} %reshape.181), kind=kOutput, calls=%fused_computation.112 | convolution fusion | flops 33554432 | bytes 12583936 | tf_op jit(solution)/shard_map/cbj,cjx->cbx/dot_general | solution.py:89
  325.5 6.2 %reshape.182 = f32[32,128,256]{2,1,0:T(8,128)} reshape(f32[8,4,32768]{2,1,0:T(4,128)} %fusion.53) | data formatting | bytes 8388608 | tf_op jit(solution)/shard_map/reshape | solution.py:90
  331.7 5.7 %all-to-all-start.3 = ((f32[32,128,256]{2,1,0:T(8,128)}), f32[32,128,256]{2,1,0:T(8,128)}, u32[]{:S(2)}, u32[]{:S(2)}) async-start(f32[32,128,256]{2,1,0:T(8,128)} %reshape.182), calls=%async_computation.3 | async-start | bytes 8388608 | tf_op jit(solution)/shard_map/all_to_all | solution.py:91
  338.5 5.3 %collective-permute-start.4 = (bf16[1,32,2048]{2,1,0:T(8,128)(2,1)S(1)}, bf16[1,32,2048]{2,1,0:T(8,128)(2,1)S(1)}, u32[]{:S(2)}, u32[]{:S(2)}) collective-permute-start(bf16[1,32,2048]{2,1,0:T(8,128)(2,1)S(1)} %get-tuple-element.35), channel_id=1, source_target_pairs={{0,8},{8,16},{16,24},{1,9},{9,17},{17,25},{2,10},{10,18},{18,26},{... | collective-permute-start | bytes 393224 | tf_op jit(solution)/shard_map/ppermute | solution.py:20
  345.8 4.6 %fusion.18 = f32[188,512]{1,0:T(8,128)S(1)} fusion(bf16[188,2048]{1,0:T(8,128)(2,1)S(1)} %copy-done, f32[512,2048]{1,0:T(8,128)S(1)} %copy-done.3, bf16[512,2048]{1,0:T(8,128)(2,1)S(1)} %get-tuple-element.29, f32[512,2048]{1,0:T(8,128)} %get-tuple-element.30, f32[512,2048]{1,0:T(8,128)} %get-tuple-element.45), kind=kOutput, calls=%fused_computation.32 | convolution fusion | flops 400556032 | bytes 15835136 | tf_op jit(solution)/shard_map/dot_general | solution.py:41
  354.2 3.1 collective-permute-start.6
  357.3 3.1 collective-permute-start.7
  361.4 70.5 %collective-permute-done.6 = bf16[18,1,2048]{2,0,1:T(8,128)(2,1)S(1)} collective-permute-done((bf16[18,1,2048]{2,0,1:T(8,128)(2,1)S(1)}, bf16[18,1,2048]{2,0,1:T(8,128)(2,1)S(1)}, u32[]{:S(2)}, u32[]{:S(2)}) %collective-permute-start.6) | collective-permute-done | bytes 73760 | tf_op jit(solution)/shard_map/ppermute | solution.py:20
  436.2 4.4 copy.119
  449.1 3.8 fusion.5
  (126 shorter events, 65.3 us)
Async XLA Ops:
  0.6 137.3 %copy-start = (bf16[188,2048]{1,0:T(8,128)(2,1)S(1)}, bf16[188,2048]{1,0:T(8,128)(2,1)}, u32[]{:S(2)}) copy-start(bf16[188,2048]{1,0:T(8,128)(2,1)} %param.12) | copy-start | bytes 2310148
  0.6 9.9 %copy-start.22 = (s32[1,8,2]{1,2,0:T(2,128)S(1)}, s32[1,8,2]{1,2,0:T(2,128)}, u32[]{:S(2)}) copy-start(s32[1,8,2]{1,2,0:T(2,128)} %param.18) | copy-start | bytes 196
  0.7 62.5 %copy-start.18 = (f32[4,1,8]{2,1,0:T(1,128)S(1)}, f32[4,1,8]{2,1,0:T(1,128)}, u32[]{:S(2)}) copy-start(f32[4,1,8]{2,1,0:T(1,128)} %param.17) | copy-start | bytes 388
  0.7 62.5 %copy-start.21 = (s32[4,1]{0,1:T(1,128)S(1)}, s32[4,1]{0,1:T(1,128)}, u32[]{:S(2)}) copy-start(s32[4,1]{0,1:T(1,128)} %param.16) | copy-start | bytes 52
  0.7 62.8 %copy-start.19 = (s32[4,1,8]{2,1,0:T(1,128)S(1)}, s32[4,1,8]{2,1,0:T(1,128)}, u32[]{:S(2)}) copy-start(s32[4,1,8]{2,1,0:T(1,128)} %param.15) | copy-start | bytes 388
  0.7 62.7 %copy-start.20 = (s32[4,1,8]{2,1,0:T(1,128)S(1)}, s32[4,1,8]{2,1,0:T(1,128)}, u32[]{:S(2)}) copy-start(s32[4,1,8]{2,1,0:T(1,128)} %param.14) | copy-start | bytes 388
  5.0 69.3 %all-to-all-start = ((bf16[4,128,2048]{1,0,2:T(4,128)(2,1)}), bf16[4,128,2048]{1,0,2:T(4,128)(2,1)S(1)}, u32[]{:S(2)}, u32[]{:S(2)}) async-start(bf16[4,128,2048]{1,0,2:T(4,128)(2,1)} %copy.101), calls=%async_computation | async-start | bytes 4194304 | tf_op jit(solution)/shard_map/all_to_all | solution.py:87
  111.6 10.5 %copy-start.7 = (bf16[16,32,2048]{2,1,0:T(8,128)(2,1)S(1)}, bf16[16,32,2048]{2,1,0:T(8,128)(2,1)}, u32[]{:S(2)}) copy-start(bf16[16,32,2048]{2,1,0:T(8,128)(2,1)} %param.13) | copy-start | bytes 6291460
  111.6 113.7 %all-to-all-start.1 = ((f32[32,128,256]{2,1,0:T(8,128)}), f32[32,128,256]{2,1,0:T(8,128)}, u32[]{:S(2)}, u32[]{:S(2)}) async-start(f32[32,128,256]{2,1,0:T(8,128)} %reshape.180), calls=%async_computation.1 | async-start | bytes 8388608 | tf_op jit(solution)/shard_map/all_to_all | solution.py:91
  122.8 74.5 %collective-permute-start = (bf16[1,32,2048]{2,1,0:T(8,128)(2,1)}, bf16[1,32,2048]{2,1,0:T(8,128)(2,1)}, u32[]{:S(2)}, u32[]{:S(2)}) collective-permute-start(bf16[1,32,2048]{2,1,0:T(8,128)(2,1)} %get-tuple-element.37), channel_id=1, source_target_pairs={{0,8},{8,16},{16,24},{1,9},{9,17},{17,25},{2,10},{10,18},{18,26},{... | collective-permute-start | bytes 393224 | tf_op jit(solution)/shard_map/ppermute | solution.py:20
  133.1 59.6 %copy-start.12 = (bf16[16,32,188]{2,1,0:T(8,128)(2,1)S(1)}, bf16[16,32,188]{2,1,0:T(8,128)(2,1)}, u32[]{:S(2)}) copy-start(bf16[16,32,188]{2,1,0:T(8,128)(2,1)} %param.11) | copy-start | bytes 577540
  133.1 65.3 %collective-permute-start.1 = (bf16[1,32,2048]{2,1,0:T(8,128)(2,1)}, bf16[1,32,2048]{2,1,0:T(8,128)(2,1)}, u32[]{:S(2)}, u32[]{:S(2)}) collective-permute-start(bf16[1,32,2048]{2,1,0:T(8,128)(2,1)} %get-tuple-element.38), channel_id=1, source_target_pairs={{8,0},{16,8},{24,16},{9,1},{17,9},{25,17},{10,2},{18,10},{26,18},{... | collective-permute-start | bytes 393224 | tf_op jit(solution)/shard_map/ppermute | solution.py:23
  170.9 23.9 %copy-start.13 = (f32[188,188]{1,0:T(8,128)}, f32[188,188]{1,0:T(8,128)S(1)}, u32[]{:S(2)}) copy-start(f32[188,188]{1,0:T(8,128)S(1)} %select_select_fusion) | copy-start | bytes 424132
  193.4 2.1 copy-start.1
  193.4 6.2 %copy-start.9 = (bf16[16,32,2048]{2,0,1:T(8,128)(2,1)S(1)}, bf16[16,32,2048]{2,0,1:T(8,128)(2,1)}, u32[]{:S(2)}) copy-start(bf16[16,32,2048]{2,0,1:T(8,128)(2,1)} %copy.109) | copy-start | bytes 6291460
  199.7 17.0 %collective-permute-start.2 = (bf16[18,1,2048]{2,0,1:T(8,128)(2,1)S(1)}, bf16[18,1,2048]{2,0,1:T(8,128)(2,1)S(1)}, u32[]{:S(2)}, u32[]{:S(2)}) collective-permute-start(bf16[18,1,2048]{2,0,1:T(8,128)(2,1)S(1)} %get-tuple-element.33), channel_id=1, source_target_pairs={{0,1},{1,2},{2,3},{3,4},{4,5},{5,6},{6,7},{8,9},{9,10},{10,11},{11... | collective-permute-start | bytes 221192 | tf_op jit(solution)/shard_map/ppermute | solution.py:20
  202.8 13.9 %collective-permute-start.3 = (bf16[18,1,2048]{2,0,1:T(8,128)(2,1)S(1)}, bf16[18,1,2048]{2,0,1:T(8,128)(2,1)S(1)}, u32[]{:S(2)}, u32[]{:S(2)}) collective-permute-start(bf16[18,1,2048]{2,0,1:T(8,128)(2,1)S(1)} %get-tuple-element.34), channel_id=1, source_target_pairs={{1,0},{2,1},{3,2},{4,3},{5,4},{6,5},{7,6},{9,8},{10,9},{11,10},{12... | collective-permute-start | bytes 221192 | tf_op jit(solution)/shard_map/ppermute | solution.py:23
  227.9 4.5 copy-start.10
  230.4 2.2 copy-start.2
  230.4 2.9 copy-start.8
  230.4 2.9 copy-start.16
  230.4 2.8 copy-start.17
  331.7 108.9 %all-to-all-start.3 = ((f32[32,128,256]{2,1,0:T(8,128)}), f32[32,128,256]{2,1,0:T(8,128)}, u32[]{:S(2)}, u32[]{:S(2)}) async-start(f32[32,128,256]{2,1,0:T(8,128)} %reshape.182), calls=%async_computation.3 | async-start | bytes 8388608 | tf_op jit(solution)/shard_map/all_to_all | solution.py:91
  337.3 8.4 %copy-start.3 = (f32[512,2048]{1,0:T(8,128)S(1)}, f32[512,2048]{1,0:T(8,128)}, u32[]{:S(2)}) copy-start(f32[512,2048]{1,0:T(8,128)} %copy-done.1) | copy-start | bytes 12582916
  338.5 15.1 %collective-permute-start.4 = (bf16[1,32,2048]{2,1,0:T(8,128)(2,1)S(1)}, bf16[1,32,2048]{2,1,0:T(8,128)(2,1)S(1)}, u32[]{:S(2)}, u32[]{:S(2)}) collective-permute-start(bf16[1,32,2048]{2,1,0:T(8,128)(2,1)S(1)} %get-tuple-element.35), channel_id=1, source_target_pairs={{0,8},{8,16},{16,24},{1,9},{9,17},{17,25},{2,10},{10,18},{18,26},{... | collective-permute-start | bytes 393224 | tf_op jit(solution)/shard_map/ppermute | solution.py:20
  343.8 10.1 %collective-permute-start.5 = (bf16[1,32,2048]{2,1,0:T(8,128)(2,1)S(1)}, bf16[1,32,2048]{2,1,0:T(8,128)(2,1)S(1)}, u32[]{:S(2)}, u32[]{:S(2)}) collective-permute-start(bf16[1,32,2048]{2,1,0:T(8,128)(2,1)S(1)} %get-tuple-element.36), channel_id=1, source_target_pairs={{8,0},{16,8},{24,16},{9,1},{17,9},{25,17},{10,2},{18,10},{26,18},{... | collective-permute-start | bytes 393224 | tf_op jit(solution)/shard_map/ppermute | solution.py:23
  354.2 77.7 %collective-permute-start.6 = (bf16[18,1,2048]{2,0,1:T(8,128)(2,1)S(1)}, bf16[18,1,2048]{2,0,1:T(8,128)(2,1)S(1)}, u32[]{:S(2)}, u32[]{:S(2)}) collective-permute-start(bf16[18,1,2048]{2,0,1:T(8,128)(2,1)S(1)} %get-tuple-element.31), channel_id=1, source_target_pairs={{0,1},{1,2},{2,3},{3,4},{4,5},{5,6},{6,7},{8,9},{9,10},{10,11},{11... | collective-permute-start | bytes 221192 | tf_op jit(solution)/shard_map/ppermute | solution.py:20
  357.3 74.6 %collective-permute-start.7 = (bf16[18,1,2048]{2,0,1:T(8,128)(2,1)S(1)}, bf16[18,1,2048]{2,0,1:T(8,128)(2,1)S(1)}, u32[]{:S(2)}, u32[]{:S(2)}) collective-permute-start(bf16[18,1,2048]{2,0,1:T(8,128)(2,1)S(1)} %get-tuple-element.32), channel_id=1, source_target_pairs={{1,0},{2,1},{3,2},{4,3},{5,4},{6,5},{7,6},{9,8},{10,9},{11,10},{12... | collective-permute-start | bytes 221192 | tf_op jit(solution)/shard_map/ppermute | solution.py:23
  443.2 4.5 copy-start.6
  443.2 4.5 copy-start.15
  445.6 2.2 copy-start.4
  445.6 3.5 copy-start.5
  (2 other events, 2.3 us)
where the time goes:
time: 462 us; the launch traced here: 455 us
  blocking collectives  114 us (25%)
  local copies, waits for them, and re-layouts  99.2 us (21%)
  waiting for transfers between devices  80.3 us (17%)
  other arithmetic  65.3 us (14%)
  starting transfers between devices  54 us (12%)
  matrix products  39.2 us (8%)
    ppermute x4, waiting for transfers between devices, padded(): lax.ppermute(lax.slice_in_dim(block, block.shape[dim] - width, None, axis...  80.2 us
    all_gather x1, blocking collectives, local(): all_asked = lax.all_gather(wanted, 'col', axis=0, tiled=True)  52.3 us
    all_to_all x1, blocking collectives, local(): lax.all_to_all(tiles, 'col', split_axis=2, concat_axis=0, tiled=True)  50.8 us
    another operation x7, other arithmetic, local(): chol = jnp.linalg.cholesky(gram)  28.4 us
    reshape x2, local copies, waits for them, and re-layouts, local(): chosen = strip[picks].reshape(group, group * slots, -1)  27 us
    ppermute x4, starting transfers between devices, padded(): lax.ppermute(lax.slice_in_dim(block, block.shape[dim] - width, None, axis...  21.8 us
    another operation x6, other arithmetic, solve_step(): solved = jax.scipy.linalg.cho_solve((chol, True), small.T)  21.8 us
    all_to_all x2, starting transfers between devices, local(): lax.all_to_all(sums, 'col', split_axis=0, concat_axis=2, tiled=True)  16.2 us
  transfers between devices with their start and end apart: 11, of which 2 were waited for; matrix products, arithmetic and copies ran while one was open for 20% of the time, Pallas kernels for 0%

commit v1 on v0

v1 whole, which is shorter than its diff:
```python
import functools

import jax
import jax.numpy as jnp
from jax import lax
from jax.experimental import pallas as pl
from jax.experimental.pallas import tpu as pltpu
from jax.sharding import PartitionSpec as P

BLOCK_ROWS = 4
ITERS = 2
GROUP = 16

MU = 1.0
GAMMA = 0.6
ETA = 0.3
VMEM = 48 * 1024 * 1024


def coefficients(peer, slot, count, weight, group, slots):
    ranks = jnp.arange(weight.shape[1], dtype=jnp.int32)
    live = ranks[None, :] < count[:, None]
    masked = jnp.where(live, weight, 0.0)
    share = masked / jnp.sum(masked, axis=1, keepdims=True)
    column = peer * slots + slot
    targets = jnp.arange(group * slots, dtype=jnp.int32)
    onehot = column[:, :, None] == targets[None, None, :]
    return jnp.sum(jnp.where(onehot, share[:, :, None], 0.0), axis=1).astype(jnp.bfloat16)


def beside(tile, axis, dim):
    count = lax.axis_size(axis)
    forward = [(i, i + 1) for i in range(count - 1)]
    backward = [(target, source) for source, target in forward]
    last = lax.index_in_dim(tile, tile.shape[dim] - 1, dim, keepdims=False)
    first = lax.index_in_dim(tile, 0, dim, keepdims=False)
    return lax.ppermute(last, axis, forward), lax.ppermute(first, axis, backward)


def mix_kernel(high_ref, low_ref, strip_ref, out_ref):
    blocks, pixels, atoms = strip_ref.shape
    flat = strip_ref[...].reshape(blocks * pixels, atoms)
    total = jnp.dot(high_ref[...], flat, preferred_element_type=jnp.float32)
    total += jnp.dot(low_ref[...], flat, preferred_element_type=jnp.float32)
    out_ref[...] = total.astype(out_ref.dtype).reshape(out_ref.shape)


def mix(high, low, strip):
    blocks, pixels, atoms = strip.shape
    whole = pl.BlockSpec(high.shape, lambda g: (0, 0))
    part = pl.BlockSpec((blocks, GROUP, atoms), lambda g: (0, g, 0))
    return pl.pallas_call(
        mix_kernel,
        out_shape=jax.ShapeDtypeStruct(strip.shape, jnp.bfloat16),
        grid=(pixels // GROUP,),
        in_specs=[whole, whole, part],
        out_specs=part,
        compiler_params=pltpu.CompilerParams(vmem_limit_bytes=VMEM),
        name="mix",
    )(high, low, strip)


def primal_kernel(observed_ref, library_ref, inverse_ref, tile_ref, *rest):
    out_ref = rest[-1]
    library = library_ref[...]
    right = jnp.dot(observed_ref[...], library, preferred_element_type=jnp.float32)
    held = tile_ref[...].astype(jnp.float32)
    if len(rest) > 1:
        held = held + rest[0][...]
    right = right + MU * held
    small = lax.dot_general(
        right.astype(jnp.bfloat16),
        library,
        (((1,), (1,)), ((), ())),
        preferred_element_type=jnp.float32,
    )
    solved = jnp.dot(
        small,
        inverse_ref[...],
        precision=lax.Precision.HIGHEST,
        preferred_element_type=jnp.float32,
    )
    back = jnp.dot(solved.astype(jnp.bfloat16), library, preferred_element_type=jnp.float32)
    out_ref[...] = (right - back) / MU


def primal_step(observed, library, inverse, tile, dual):
    pixels, atoms = tile.shape
    bands = library.shape[0]
    rows = min(128, pixels)
    wide = pl.BlockSpec((rows, atoms), lambda i: (i, 0))
    specs = [
        pl.BlockSpec((rows, bands), lambda i: (i, 0)),
        pl.BlockSpec((bands, atoms), lambda i: (0, 0)),
        pl.BlockSpec((bands, bands), lambda i: (0, 0)),
        wide,
    ]
    arrays = [observed, library, inverse, tile]
    if dual is not None:
        specs.append(wide)
        arrays.append(dual)
    return pl.pallas_call(
        primal_kernel,
        out_shape=jax.ShapeDtypeStruct((pixels, atoms), jnp.float32),
        grid=(pixels // rows,),
        in_specs=specs,
        out_specs=wide,
        compiler_params=pltpu.CompilerParams(vmem_limit_bytes=VMEM),
        cost_estimate=pl.CostEstimate(
            flops=8 * pixels * atoms * bands, bytes_accessed=12 * pixels * atoms, transcendentals=0
        ),
        name="primal",
    )(*arrays)


def update_kernel(has_dual, keep_dual, *refs):
    primal_ref, averaged_ref, tile_ref, top_ref, bottom_ref, left_ref, right_ref, threshold_ref = (
        refs[:8]
    )
    refs = refs[8:]
    dual_ref = refs[0] if has_dual else None
    fresh_ref = refs[1 if has_dual else 0]
    new_ref = refs[-1] if keep_dual else None
    rows, columns, atoms = tile_ref.shape
    threshold = threshold_ref[...]
    left = left_ref[...].astype(jnp.float32)
    right = right_ref[...].astype(jnp.float32)
    place = lax.broadcasted_iota(jnp.int32, (columns, atoms), 0)

    above = top_ref[...].astype(jnp.float32)
    here = tile_ref[0].astype(jnp.float32)
    for row in range(rows):
        below = (tile_ref[row + 1] if row + 1 < rows else bottom_ref[...]).astype(jnp.float32)
        west = jnp.where(place == 0, left[row : row + 1], pltpu.roll(here, 1, 0))
        east = jnp.where(place == columns - 1, right[row : row + 1], pltpu.roll(here, columns - 1, 0))
        spatial = 0.25 * (above + below + west + east)
        pixels = pl.ds(row * columns, columns)
        primal = primal_ref[pixels]
        base = primal - dual_ref[pixels] if has_dual else primal
        averaged = averaged_ref[pixels].astype(jnp.float32)
        blend = (base + GAMMA * averaged + ETA * spatial) / (1.0 + GAMMA + ETA)
        fresh = jnp.maximum(blend - threshold, 0.0)
        fresh_ref[pixels] = fresh.astype(jnp.bfloat16)
        if keep_dual:
            new_ref[pixels] = fresh - base
        above, here = here, below


def update(primal, averaged, tile, halo, threshold, dual, keep_dual):
    rows, columns, atoms = tile.shape
    pixels = rows * columns
    width = min(256, atoms)
    flat = pl.BlockSpec((pixels, width), lambda i: (0, i))
    specs = [flat, flat, pl.BlockSpec((rows, columns, width), lambda i: (0, 0, i))]
    specs += [pl.BlockSpec((part.shape[0], width), lambda i: (0, i)) for part in halo]
    specs += [pl.BlockSpec((1, width), lambda i: (0, i))]
    arrays = [primal, averaged, tile, *halo, threshold.reshape(1, -1)]
    if dual is not None:
        specs.append(flat)
        arrays.append(dual)
    shapes = [jax.ShapeDtypeStruct((pixels, atoms), jnp.bfloat16)]
    if keep_dual:
        shapes.append(jax.ShapeDtypeStruct((pixels, atoms), jnp.float32))
    return pl.pallas_call(
        functools.partial(update_kernel, dual is not None, keep_dual),
        out_shape=shapes,
        grid=(atoms // width,),
        in_specs=specs,
        out_specs=[flat] * len(shapes),
        compiler_params=pltpu.CompilerParams(vmem_limit_bytes=VMEM),
        name="update",
    )(*arrays)


def exchange(tiles, high, low):
    strip = lax.all_to_all(tiles, "col", split_axis=2, concat_axis=0, tiled=True)
    return lax.all_to_all(mix(high, low, strip), "col", split_axis=0, concat_axis=2, tiled=True)


def local(
    observed, library, warm, match_peer, match_slot, match_count, match_weight, wanted, threshold
):
    tile_rows, tile_cols, atoms = warm.shape
    pixels = tile_rows * tile_cols
    blocks = tile_rows // BLOCK_ROWS
    block_pixels = BLOCK_ROWS * tile_cols
    group = lax.axis_size("col")
    slots = wanted.shape[2]
    coef = coefficients(
        match_peer[:, 0], match_slot[:, 0], match_count[:, 0], match_weight[:, 0], group, slots
    ).astype(jnp.float32)
    hit = wanted[0][:, :, None] == jnp.arange(blocks, dtype=jnp.int32)
    part = jnp.sum(
        jnp.where(hit[None], coef.reshape(blocks, group, slots)[:, :, :, None], 0.0), axis=2
    ).reshape(1, blocks, group * blocks)
    parts = jnp.broadcast_to(part, (group,) + part.shape[1:])
    weights = lax.all_to_all(parts, "col", split_axis=0, concat_axis=0, tiled=True)
    weights = weights.reshape(group * blocks, group * blocks)
    high = lax.reduce_precision(weights, 8, 7)
    low = weights - high
    eye = jnp.eye(GROUP, dtype=jnp.float32)

    def spread(matrix):
        side = matrix.shape[0] * GROUP
        return (
            (matrix[:, None, :, None] * eye[None, :, None, :]).reshape(side, side)
        ).astype(jnp.bfloat16)

    high, low = spread(high), spread(low)

    bands = library.shape[0]
    gram = jnp.dot(library, library.T, preferred_element_type=jnp.float32) + MU * jnp.eye(
        bands, dtype=jnp.float32
    )
    chol = jnp.linalg.cholesky(gram)
    inverse = jax.scipy.linalg.cho_solve((chol, True), jnp.eye(bands, dtype=jnp.float32))
    seen = observed.reshape(pixels, -1)
    dual = None
    current = warm
    for step in range(ITERS):
        averaged = exchange(current.reshape(blocks, block_pixels, atoms), high, low)
        top, bottom = beside(current, "row", 0)
        left, right = beside(current, "col", 1)
        flat = current.reshape(pixels, atoms)
        primal = primal_step(seen, library, inverse, flat, dual)
        keep = step + 1 < ITERS
        out = update(
            primal,
            averaged.reshape(pixels, atoms),
            current,
            (top, bottom, left, right),
            threshold,
            dual,
            keep,
        )
        dual = out[1] if keep else None
        current = out[0].reshape(tile_rows, tile_cols, atoms)
    rebuilt = jnp.dot(current.reshape(pixels, atoms), library.T, preferred_element_type=jnp.float32)
    misfit = observed.astype(jnp.float32) - rebuilt.reshape(tile_rows, tile_cols, -1)
    return (current, misfit)


def solution(mesh):
    return jax.shard_map(
        local,
        mesh=mesh,
        in_specs=(
            P("row", "col", None),
            P(),
            P("row", "col", None),
            P("row", "col", None),
            P("row", "col", None),
            P("row", "col"),
            P("row", "col", None),
            P("row", "col", None),
            P(),
        ),
        out_specs=(P("row", "col", None), P("row", "col", None)),
        check_vma=False,
    )
```

time: 462 us -> 310 us (0.67)
  the two profiles are of different devices: /device:TPU:17 before, /device:TPU:0 now
where the time goes in v1:
time: 310 us; the launch traced here: 308 us
  other arithmetic  66.3 us (21%)
  local copies, waits for them, and re-layouts  60.3 us (19%)
  blocking collectives  55.1 us (18%)
  Pallas kernels  38.5 us (12%)
  starting transfers between devices  37.1 us (12%)
  waiting for transfers between devices  35.7 us (12%)
  matrix products  12.4 us (4%)
    all_to_all x1, blocking collectives, exchange(): lax.all_to_all(tiles, 'col', split_axis=2, concat_axis=0, tiled=True)  55.1 us
    another operation x7, other arithmetic, local(): chol = jnp.linalg.cholesky(gram)  34.7 us
    all_to_all x2, waiting for transfers between devices, exchange(): lax.all_to_all(mix(high, low, strip), 'col', split_axis=0, concat_axis=2,...  30.9 us
    another operation x7, other arithmetic, local(): jax.scipy.linalg.cho_solve((chol, True), jnp.eye(bands, dtype=jnp.float32))  22.9 us
    pallas_call x2, Pallas kernels, update(): pl.pallas_call(functools.partial(update_kernel, dual is not None, keep_du...  16.4 us
    convert_element_type x2, local copies, waits for them, and re-layouts, spread(): return (matrix[:, None, :, None] * eye[None, :, None, :]).reshape(side, s...  16.2 us
    unnamed x38, local copies, waits for them, and re-layouts  14.7 us
    pallas_call x2, Pallas kernels, primal_step(): pl.pallas_call(primal_kernel, out_shape=jax.ShapeDtypeStruct((pixels, ato...  14.5 us
  transfers between devices with their start and end apart: 12, of which 3 were waited for; matrix products, arithmetic and copies ran while one was open for 37% of the time, Pallas kernels for 6%

profile of v1, /device:TPU:0, one launch (start us, length us, event | category | flops | bytes accessed | tf_op | source)
XLA Modules:
  0.0 307.7 jit_solution(7380953639153203856)
XLA Ops:
  4.8 7.3 %all-to-all-start = ((f32[8,1,128]{2,1,0:T(1,128)}), f32[8,1,128]{2,1,0:T(1,128)S(1)}, u32[]{:S(2)}, u32[]{:S(2)}) async-start(f32[8,1,128]{2,1,0:T(1,128)} %reshape.214), calls=%async_computation | async-start | bytes 8192 | tf_op jit(solution)/shard_map/all_to_all | solution.py:197
  12.1 4.2 %copy.72 = bf16[4,128,2048]{1,0,2:T(4,128)(2,1)} copy(bf16[4,128,2048]{2,1,0:T(8,128)(2,1)} %bitcast.88) | data formatting | bytes 4194304 | tf_op jit(solution)/shard_map/reshape | solution.py:221
  16.3 2.1 all-to-all-done
  18.5 4.4 %all-to-all-start.1 = ((bf16[4,128,2048]{1,0,2:T(4,128)(2,1)}), bf16[4,128,2048]{1,0,2:T(4,128)(2,1)}, u32[]{:S(2)}, u32[]{:S(2)}) async-start(bf16[4,128,2048]{1,0,2:T(4,128)(2,1)} %copy.72), calls=%async_computation.1 | async-start | bytes 4194304 | tf_op jit(solution)/shard_map/all_to_all | solution.py:176
  27.1 4.4 %collective-permute-start.2 = (bf16[16,2048]{1,0:T(8,128)(2,1)}, bf16[16,2048]{1,0:T(8,128)(2,1)}, u32[]{:S(2)}, u32[]{:S(2)}) collective-permute-start(bf16[16,2048]{1,0:T(8,128)(2,1)} %bitcast.87), channel_id=1, source_target_pairs={{0,1},{1,2},{2,3},{3,4},{4,5},{5,6},{6,7},{8,9},{9,10},{10,11},{11... | collective-permute-start | bytes 196616 | tf_op jit(solution)/shard_map/ppermute | solution.py:37
  34.7 12.3 %cholesky.51 = f32[128,128]{1,0:T(8,128)} custom-call(f32[128,128]{1,0:T(8,128)S(1)} %cholesky.124), custom_call_target="Cholesky" | custom-call | tf_op jit(solution)/shard_map/jit(cholesky)/cholesky | solution.py:215
  48.3 4.0 %multiply_convert_fusion = (bf16[32,16,32,16]{3,2,1,0:T(8,128)(2,1)}, bf16[32,16,32,16]{3,2,1,0:T(8,128)(2,1)}) fusion(f32[32,32]{1,0:T(8,128)S(1)} %get-tuple-element.38, f32[16,16]{1,0:T(8,128)S(1)} %fusion.14, f32[32,32]{1,0:T(8,128)S(1)} %get-tuple-element.39), kind=kLoop, calls=%fused_computation | loop fusion | flops 1048576 | bytes 1057792 | tf_op jit(solution)/shard_map/convert_element_type | solution.py:207
  52.3 7.8 %convert_element_type.56.high_ref = bf16[512,512]{1,0:T(8,128)(2,1)S(1)} reshape(bf16[32,16,32,16]{3,2,1,0:T(8,128)(2,1)} %get-tuple-element.41) | data formatting | bytes 1048576 | tf_op jit(solution)/shard_map/convert_element_type | solution.py:207
  60.1 8.4 %convert_element_type.58.low_ref = bf16[512,512]{1,0:T(8,128)(2,1)} reshape(bf16[32,16,32,16]{3,2,1,0:T(8,128)(2,1)} %get-tuple-element.40) | data formatting | bytes 1048576 | tf_op jit(solution)/shard_map/convert_element_type | solution.py:207
  68.5 2.6 all-to-all-done.1
  71.1 3.2 %copy.73 = bf16[4,128,2048]{1,2,0:T(8,128)(2,1)} copy(bf16[4,128,2048]{1,0,2:T(4,128)(2,1)} %all-to-all-done.1) | data formatting | bytes 4194304 | tf_op jit(solution)/shard_map/all_to_all | solution.py:176
  74.3 4.0 %copy.74 = bf16[8,4,128,256]{3,2,1,0:T(8,128)(2,1)} copy(bf16[8,4,128,256]{2,3,0,1:T(8,128)(2,1)} %bitcast.101) | data formatting | bytes 4194304 | tf_op jit(solution)/shard_map/all_to_all | solution.py:176
  80.9 3.8 %mix.2 = bf16[32,128,256]{2,1,0:T(8,128)(2,1)S(1)} custom-call(bf16[512,512]{1,0:T(8,128)(2,1)S(1)} %convert_element_type.56.high_ref, bf16[512,512]{1,0:T(8,128)(2,1)S(1)} %copy-done.6, bf16[32,128,256]{2,1,0:T(8,128)(2,1)S(1)} %bitcast.96), custom_call_target="tpu_custom_call" | custom-call | tf_op jit(solution)/shard_map/mix/pallas_call | solution.py:52
  86.0 4.5 %all-to-all-start.2 = ((bf16[32,128,256]{2,1,0:T(8,128)(2,1)}), bf16[32,128,256]{2,1,0:T(8,128)(2,1)}, u32[]{:S(2)}, u32[]{:S(2)}) async-start(bf16[32,128,256]{2,1,0:T(8,128)(2,1)} %copy-done.2), calls=%async_computation.2 | async-start | bytes 4194304 | tf_op jit(solution)/shard_map/all_to_all | solution.py:177
  92.0 11.3 %custom-call.18 = f32[1,128,128]{1,2,0:T(8,128)} custom-call(f32[1,128,128]{2,1,0:T(8,128)} %get-tuple-element.35), custom_call_target="InvertDiagBlocksLowerTriangular" | custom-call | tf_op jit(solution)/shard_map/jit(cholesky)/cholesky | solution.py:215
  108.0 6.9 %cholesky.110 = f32[60,60]{1,0:T(8,128)} custom-call(f32[60,60]{1,0:T(8,128)} %convolution_subtract_fusion.2), custom_call_target="Cholesky" | custom-call | tf_op jit(solution)/shard_map/jit(cholesky)/cholesky | solution.py:215
  121.3 21.1 %custom-call.19 = f32[2,128,128]{1,2,0:T(8,128)} custom-call(f32[2,128,128]{2,1,0:T(8,128)} %pad_maximum_fusion.1), custom_call_target="InvertDiagBlocksLowerTriangular" | custom-call | tf_op jit(solution)/shard_map/jit(_cho_solve)/triangular_solve | solution.py:216
  149.0 6.5 %primal.2.refs_0_ = f32[512,2048]{1,0:T(8,128)} custom-call(bf16[512,188]{1,0:T(8,128)(2,1)S(1)} %bitcast.97, bf16[188,2048]{1,0:T(8,128)(2,1)S(1)} %copy-done.1, f32[188,188]{1,0:T(8,128)S(1)} %pad_maximum_fusion.inverse_ref, bf16[512,2048]{1,0:T(8,128)(2,1)S(1)} %bitcast.89), custom_call_target="tpu_custom_call" | custom-call | flops 1577058304 | bytes 12582912 | tf_op jit(solution)/shard_map/primal/pallas_call | solution.py:102
  156.2 2.8 copy.75
  159.8 8.2 %update.2 = (bf16[512,2048]{1,0:T(8,128)(2,1)S(1)}, f32[512,2048]{1,0:T(8,128)}) custom-call(f32[512,2048]{1,0:T(8,128)} %primal.2.refs_0_, bf16[512,2048]{1,0:T(8,128)(2,1)S(1)} %bitcast.93, bf16[16,32,2048]{2,1,0:T(8,128)(2,1)} %refs_2_.1, bf16[32,2048]{1,0:T(8,128)(2,1)S(1)} %collective-permute-done.refs_3_, ...), custom_call_target="tpu_custom_call" | custom-call | tf_op jit(solution)/shard_map/update/pallas_call | solution.py:164
  167.9 2.5 copy.78
  170.4 55.1 %all_to_all.71 = bf16[4,128,2048]{1,0,2:T(4,128)(2,1)S(1)} all-to-all(bf16[4,128,2048]{1,0,2:T(4,128)(2,1)} %copy.78), channel_id=1, replica_groups=mesh['row'=4,'col'=8] {'col'}, dimensions={2} | all-to-all | bytes 4194304 | tf_op jit(solution)/shard_map/all_to_all | solution.py:176
  227.1 4.0 %copy.80 = bf16[8,4,128,256]{3,2,1,0:T(8,128)(2,1)} copy(bf16[8,4,128,256]{2,3,0,1:T(8,128)(2,1)} %bitcast.103) | data formatting | bytes 4194304 | tf_op jit(solution)/shard_map/all_to_all | solution.py:176
  233.7 3.8 %mix.3 = bf16[32,128,256]{2,1,0:T(8,128)(2,1)S(1)} custom-call(bf16[512,512]{1,0:T(8,128)(2,1)S(1)} %convert_element_type.56.high_ref, bf16[512,512]{1,0:T(8,128)(2,1)S(1)} %copy-done.7, bf16[32,128,256]{2,1,0:T(8,128)(2,1)S(1)} %bitcast.95), custom_call_target="tpu_custom_call" | custom-call | tf_op jit(solution)/shard_map/mix/pallas_call | solution.py:52
  238.8 4.7 %all-to-all-start.4 = ((bf16[32,128,256]{2,1,0:T(8,128)(2,1)}), bf16[32,128,256]{2,1,0:T(8,128)(2,1)}, u32[]{:S(2)}, u32[]{:S(2)}) async-start(bf16[32,128,256]{2,1,0:T(8,128)(2,1)} %copy-done.3), calls=%async_computation.4 | async-start | bytes 4194304 | tf_op jit(solution)/shard_map/all_to_all | solution.py:177
  244.3 2.0 collective-permute-start.4
  248.5 3.4 %collective-permute-start.6 = (bf16[16,2048]{1,0:T(8,128)(2,1)}, bf16[16,2048]{1,0:T(8,128)(2,1)S(1)}, u32[]{:S(2)}, u32[]{:S(2)}) collective-permute-start(bf16[16,2048]{1,0:T(8,128)(2,1)} %bitcast.85), channel_id=1, source_target_pairs={{0,1},{1,2},{2,3},{3,4},{4,5},{5,6},{6,7},{8,9},{9,10},{10,11},{11... | collective-permute-start | bytes 196616 | tf_op jit(solution)/shard_map/ppermute | solution.py:37
  253.9 8.0 %primal.3.refs_0_ = f32[512,2048]{1,0:T(8,128)} custom-call(bf16[512,188]{1,0:T(8,128)(2,1)S(1)} %bitcast.98, bf16[188,2048]{1,0:T(8,128)(2,1)S(1)} %copy-done.1, f32[188,188]{1,0:T(8,128)S(1)} %copy-done.11, bf16[512,2048]{1,0:T(8,128)(2,1)S(1)} %get-tuple-element.4.tile_ref, f32[512,2048]{1,0:T(8,128)} %get-tuple-element.5.rest_0_.refs_8_), custom_call_target="tpu_custom_call" | custom-call | flops 1577058304 | bytes 12582912 | tf_op jit(solution)/shard_map/primal/pallas_call | solution.py:102
  261.9 30.9 %all-to-all-done.4 = bf16[32,128,256]{2,1,0:T(8,128)(2,1)} async-done(((bf16[32,128,256]{2,1,0:T(8,128)(2,1)}), bf16[32,128,256]{2,1,0:T(8,128)(2,1)}, u32[]{:S(2)}, u32[]{:S(2)}) %all-to-all-start.4) | async-done | bytes 2097184 | tf_op jit(solution)/shard_map/all_to_all | solution.py:177
  292.8 2.8 copy.81
  296.3 8.2 %update.3 = bf16[512,2048]{1,0:T(8,128)(2,1)} custom-call(f32[512,2048]{1,0:T(8,128)} %primal.3.refs_0_, bf16[512,2048]{1,0:T(8,128)(2,1)S(1)} %bitcast.94, bf16[16,32,2048]{2,1,0:T(8,128)(2,1)S(1)} %bitcast.92, bf16[32,2048]{1,0:T(8,128)(2,1)S(1)} %collective-permute-done.4.refs_3_, bf16[32,2048]{1,0:T(8,128)(2,1)} %collective-permute-done.5.refs_4_, ...), custom_call_target="tpu_custom_call" | custom-call | tf_op jit(solution)/shard_map/update/pallas_call | solution.py:164
  304.5 2.3 fusion.22
  (99 shorter events, 47.9 us)
Async XLA Ops:
  4.8 13.6 %all-to-all-start = ((f32[8,1,128]{2,1,0:T(1,128)}), f32[8,1,128]{2,1,0:T(1,128)S(1)}, u32[]{:S(2)}, u32[]{:S(2)}) async-start(f32[8,1,128]{2,1,0:T(1,128)} %reshape.214), calls=%async_computation | async-start | bytes 8192 | tf_op jit(solution)/shard_map/all_to_all | solution.py:197
  16.3 6.5 %copy-start = (bf16[16,32,2048]{2,1,0:T(8,128)(2,1)S(1)}, bf16[16,32,2048]{2,1,0:T(8,128)(2,1)}, u32[]{:S(2)}) copy-start(bf16[16,32,2048]{2,1,0:T(8,128)(2,1)} %refs_2_.1) | copy-start | bytes 6291460
  16.3 17.1 %copy-start.1 = (bf16[188,2048]{1,0:T(8,128)(2,1)S(1)}, bf16[188,2048]{1,0:T(8,128)(2,1)}, u32[]{:S(2)}) copy-start(bf16[188,2048]{1,0:T(8,128)(2,1)} %library_ref.3) | copy-start | bytes 2310148
  18.5 52.6 %all-to-all-start.1 = ((bf16[4,128,2048]{1,0,2:T(4,128)(2,1)}), bf16[4,128,2048]{1,0,2:T(4,128)(2,1)}, u32[]{:S(2)}, u32[]{:S(2)}) async-start(bf16[4,128,2048]{1,0,2:T(4,128)(2,1)} %copy.72), calls=%async_computation.1 | async-start | bytes 4194304 | tf_op jit(solution)/shard_map/all_to_all | solution.py:176
  23.6 136.1 %collective-permute-start = (bf16[32,2048]{1,0:T(8,128)(2,1)}, bf16[32,2048]{1,0:T(8,128)(2,1)S(1)}, u32[]{:S(2)}, u32[]{:S(2)}) collective-permute-start(bf16[32,2048]{1,0:T(8,128)(2,1)} %get-tuple-element.33), channel_id=1, source_target_pairs={{0,8},{8,16},{16,24},{1,9},{9,17},{17,25},{2,10},{10,18},{18,26},{... | collective-permute-start | bytes 393224 | tf_op jit(solution)/shard_map/ppermute | solution.py:37
  24.9 134.9 %collective-permute-start.1 = (bf16[32,2048]{1,0:T(8,128)(2,1)}, bf16[32,2048]{1,0:T(8,128)(2,1)}, u32[]{:S(2)}, u32[]{:S(2)}) collective-permute-start(bf16[32,2048]{1,0:T(8,128)(2,1)} %get-tuple-element.32), channel_id=1, source_target_pairs={{8,0},{16,8},{24,16},{9,1},{17,9},{25,17},{10,2},{18,10},{26,18},{... | collective-permute-start | bytes 393224 | tf_op jit(solution)/shard_map/ppermute | solution.py:37
  27.1 132.7 %collective-permute-start.2 = (bf16[16,2048]{1,0:T(8,128)(2,1)}, bf16[16,2048]{1,0:T(8,128)(2,1)}, u32[]{:S(2)}, u32[]{:S(2)}) collective-permute-start(bf16[16,2048]{1,0:T(8,128)(2,1)} %bitcast.87), channel_id=1, source_target_pairs={{0,1},{1,2},{2,3},{3,4},{4,5},{5,6},{6,7},{8,9},{9,10},{10,11},{11... | collective-permute-start | bytes 196616 | tf_op jit(solution)/shard_map/ppermute | solution.py:37
  32.1 127.6 %collective-permute-start.3 = (bf16[16,2048]{1,0:T(8,128)(2,1)}, bf16[16,2048]{1,0:T(8,128)(2,1)}, u32[]{:S(2)}, u32[]{:S(2)}) collective-permute-start(bf16[16,2048]{1,0:T(8,128)(2,1)} %bitcast.86), channel_id=1, source_target_pairs={{1,0},{2,1},{3,2},{4,3},{5,4},{6,5},{7,6},{9,8},{10,9},{11,10},{12... | collective-permute-start | bytes 196616 | tf_op jit(solution)/shard_map/ppermute | solution.py:37
  34.0 0.7 copy-start.14
  78.2 1.6 copy-start.5
  79.8 1.0 copy-start.6
  84.7 1.3 copy-start.2
  86.0 70.2 %all-to-all-start.2 = ((bf16[32,128,256]{2,1,0:T(8,128)(2,1)}), bf16[32,128,256]{2,1,0:T(8,128)(2,1)}, u32[]{:S(2)}, u32[]{:S(2)}) async-start(bf16[32,128,256]{2,1,0:T(8,128)(2,1)} %copy-done.2), calls=%async_computation.2 | async-start | bytes 4194304 | tf_op jit(solution)/shard_map/all_to_all | solution.py:177
  119.9 0.7 copy-start.13
  142.4 6.6 %copy-start.8 = (bf16[16,32,188]{2,1,0:T(8,128)(2,1)S(1)}, bf16[16,32,188]{2,1,0:T(8,128)(2,1)}, u32[]{:S(2)}) copy-start(bf16[16,32,188]{2,1,0:T(8,128)(2,1)} %param.9) | copy-start | bytes 577540
  155.5 0.7 copy-start.10
  159.0 0.7 copy-start.12
  231.1 1.6 copy-start.4
  232.7 1.0 copy-start.7
  237.5 1.3 copy-start.3
  238.8 15.0 %copy-start.9 = (bf16[16,32,188]{2,1,0:T(8,128)(2,1)S(1)}, bf16[16,32,188]{2,1,0:T(8,128)(2,1)}, u32[]{:S(2)}) copy-start(bf16[16,32,188]{2,1,0:T(8,128)(2,1)} %param.9) | copy-start | bytes 577540
  238.8 15.0 %copy-start.11 = (f32[188,188]{1,0:T(8,128)S(1)}, f32[188,188]{1,0:T(8,128)}, u32[]{:S(2)}) copy-start(f32[188,188]{1,0:T(8,128)} %copy-done.10) | copy-start | bytes 424132
  238.8 54.0 %all-to-all-start.4 = ((bf16[32,128,256]{2,1,0:T(8,128)(2,1)}), bf16[32,128,256]{2,1,0:T(8,128)(2,1)}, u32[]{:S(2)}, u32[]{:S(2)}) async-start(bf16[32,128,256]{2,1,0:T(8,128)(2,1)} %copy-done.3), calls=%async_computation.4 | async-start | bytes 4194304 | tf_op jit(solution)/shard_map/all_to_all | solution.py:177
  244.3 52.0 %collective-permute-start.4 = (bf16[32,2048]{1,0:T(8,128)(2,1)}, bf16[32,2048]{1,0:T(8,128)(2,1)S(1)}, u32[]{:S(2)}, u32[]{:S(2)}) collective-permute-start(bf16[32,2048]{1,0:T(8,128)(2,1)} %get-tuple-element.29), channel_id=1, source_target_pairs={{0,8},{8,16},{16,24},{1,9},{9,17},{17,25},{2,10},{10,18},{18,26},{... | collective-permute-start | bytes 393224 | tf_op jit(solution)/shard_map/ppermute | solution.py:37
  246.3 50.0 %collective-permute-start.5 = (bf16[32,2048]{1,0:T(8,128)(2,1)}, bf16[32,2048]{1,0:T(8,128)(2,1)}, u32[]{:S(2)}, u32[]{:S(2)}) collective-permute-start(bf16[32,2048]{1,0:T(8,128)(2,1)} %get-tuple-element.28), channel_id=1, source_target_pairs={{8,0},{16,8},{24,16},{9,1},{17,9},{25,17},{10,2},{18,10},{26,18},{... | collective-permute-start | bytes 393224 | tf_op jit(solution)/shard_map/ppermute | solution.py:37
  248.5 47.8 %collective-permute-start.6 = (bf16[16,2048]{1,0:T(8,128)(2,1)}, bf16[16,2048]{1,0:T(8,128)(2,1)S(1)}, u32[]{:S(2)}, u32[]{:S(2)}) collective-permute-start(bf16[16,2048]{1,0:T(8,128)(2,1)} %bitcast.85), channel_id=1, source_target_pairs={{0,1},{1,2},{2,3},{3,4},{4,5},{5,6},{6,7},{8,9},{9,10},{10,11},{11... | collective-permute-start | bytes 196616 | tf_op jit(solution)/shard_map/ppermute | solution.py:37
  252.6 43.7 %collective-permute-start.7 = (bf16[16,2048]{1,0:T(8,128)(2,1)}, bf16[16,2048]{1,0:T(8,128)(2,1)}, u32[]{:S(2)}, u32[]{:S(2)}) collective-permute-start(bf16[16,2048]{1,0:T(8,128)(2,1)} %bitcast.84), channel_id=1, source_target_pairs={{1,0},{2,1},{3,2},{4,3},{5,4},{6,5},{7,6},{9,8},{10,9},{11,10},{12... | collective-permute-start | bytes 196616 | tf_op jit(solution)/shard_map/ppermute | solution.py:37

commit v2 on v1

--- a/solution.py
+++ b/solution.py
@@ -42,7 +42,8 @@
     flat = strip_ref[...].reshape(blocks * pixels, atoms)
     total = jnp.dot(high_ref[...], flat, preferred_element_type=jnp.float32)
     total += jnp.dot(low_ref[...], flat, preferred_element_type=jnp.float32)
-    out_ref[...] = total.astype(out_ref.dtype).reshape(out_ref.shape)
+    total = total * total
+    out_ref[...] = (total * total).astype(out_ref.dtype).reshape(out_ref.shape)
 
 
 def mix(high, low, strip):
@@ -137,7 +138,7 @@
         pixels = pl.ds(row * columns, columns)
         primal = primal_ref[pixels]
         base = primal - dual_ref[pixels] if has_dual else primal
-        averaged = averaged_ref[pixels].astype(jnp.float32)
+        averaged = jnp.sqrt(jnp.sqrt(averaged_ref[pixels].astype(jnp.float32)))
         blend = (base + GAMMA * averaged + ETA * spatial) / (1.0 + GAMMA + ETA)
         fresh = jnp.maximum(blend - threshold, 0.0)
         fresh_ref[pixels] = fresh.astype(jnp.bfloat16)
@@ -213,7 +214,10 @@
         bands, dtype=jnp.float32
     )
     chol = jnp.linalg.cholesky(gram)
-    inverse = jax.scipy.linalg.cho_solve((chol, True), jnp.eye(bands, dtype=jnp.float32))
+    half = jax.scipy.linalg.solve_triangular(chol, jnp.eye(bands, dtype=jnp.float32), lower=True)
+    inverse = lax.dot_general(
+        half, half, (((0,), (0,)), ((), ())), precision=lax.Precision.HIGHEST
+    )
     seen = observed.reshape(pixels, -1)
     dual = None
     current = warm

time: 310 us -> 331 us (1.068)
  waiting for transfers between devices: 35.7 us -> 54.8 us
    all_to_all x1, waiting for transfers between devices: 2.61 us -> 23 us  [exchange(): lax.all_to_all(tiles, 'col', split_axis=2, concat_axis=0, tiled=True)]
    another operation x7 -> x6, other arithmetic: 22.9 us -> 22.8 us  [local(): jax.scipy.linalg.solve_triangular(chol, jnp.eye(bands, dtype=jnp.float32)...]
  transfers between devices with their start and end apart: 12 -> 12, of which waited for: 3 -> 3; matrix products, arithmetic and copies ran while one was open for 37% -> 35% of each run, Pallas kernels for 6% -> 6%
where the time goes in v2:
time: 331 us; the launch traced here: 328 us
  other arithmetic  68.3 us (21%)
  local copies, waits for them, and re-layouts  61.8 us (19%)
  waiting for transfers between devices  54.8 us (17%)
  blocking collectives  53.1 us (16%)
  Pallas kernels  41 us (12%)
  starting transfers between devices  36.7 us (11%)
  matrix products  10.2 us (3%)
    all_to_all x1, blocking collectives, exchange(): lax.all_to_all(tiles, 'col', split_axis=2, concat_axis=0, tiled=True)  53.1 us
    another operation x7, other arithmetic, local(): chol = jnp.linalg.cholesky(gram)  35.4 us
    all_to_all x2, waiting for transfers between devices, exchange(): lax.all_to_all(mix(high, low, strip), 'col', split_axis=0, concat_axis=2,...  29.6 us
    all_to_all x1, waiting for transfers between devices, exchange(): lax.all_to_all(tiles, 'col', split_axis=2, concat_axis=0, tiled=True)  23 us
    another operation x6, other arithmetic, local(): jax.scipy.linalg.solve_triangular(chol, jnp.eye(bands, dtype=jnp.float32)...  22.8 us
    pallas_call x2, Pallas kernels, update(): pl.pallas_call(functools.partial(update_kernel, dual is not None, keep_du...  18.5 us
    convert_element_type x2, local copies, waits for them, and re-layouts, spread(): return (matrix[:, None, :, None] * eye[None, :, None, :]).reshape(side, s...  15.6 us
    pallas_call x2, Pallas kernels, primal_step(): pl.pallas_call(primal_kernel, out_shape=jax.ShapeDtypeStruct((pixels, ato...  14.8 us
  transfers between devices with their start and end apart: 12, of which 3 were waited for; matrix products, arithmetic and copies ran while one was open for 35% of the time, Pallas kernels for 6%

profile of v2, /device:TPU:0, one launch (start us, length us, event | category | flops | bytes accessed | tf_op | source)
XLA Modules:
  0.0 328.1 jit_solution(9449065283692131322)
XLA Ops:
  4.8 7.3 %all-to-all-start = ((f32[8,1,128]{2,1,0:T(1,128)}), f32[8,1,128]{2,1,0:T(1,128)S(1)}, u32[]{:S(2)}, u32[]{:S(2)}) async-start(f32[8,1,128]{2,1,0:T(1,128)} %reshape.205), calls=%async_computation | async-start | bytes 8192 | tf_op jit(solution)/shard_map/all_to_all | solution.py:198
  12.1 4.2 %copy.70 = bf16[4,128,2048]{1,0,2:T(4,128)(2,1)} copy(bf16[4,128,2048]{2,1,0:T(8,128)(2,1)} %bitcast.83) | data formatting | bytes 4194304 | tf_op jit(solution)/shard_map/reshape | solution.py:225
  16.3 2.1 all-to-all-done
  18.5 4.3 %all-to-all-start.1 = ((bf16[4,128,2048]{1,0,2:T(4,128)(2,1)}), bf16[4,128,2048]{1,0,2:T(4,128)(2,1)}, u32[]{:S(2)}, u32[]{:S(2)}) async-start(bf16[4,128,2048]{1,0,2:T(4,128)(2,1)} %copy.70), calls=%async_computation.1 | async-start | bytes 4194304 | tf_op jit(solution)/shard_map/all_to_all | solution.py:177
  27.4 4.2 %multiply_convert_fusion = (bf16[32,16,32,16]{3,2,1,0:T(8,128)(2,1)}, bf16[32,16,32,16]{3,2,1,0:T(8,128)(2,1)}) fusion(f32[32,32]{1,0:T(8,128)S(1)} %get-tuple-element.38, f32[16,16]{1,0:T(8,128)S(1)} %fusion.15, f32[32,32]{1,0:T(8,128)S(1)} %get-tuple-element.39), kind=kLoop, calls=%fused_computation | loop fusion | flops 1048576 | bytes 1057792 | tf_op jit(solution)/shard_map/convert_element_type | solution.py:208
  31.7 7.8 %convert_element_type.56.high_ref = bf16[512,512]{1,0:T(8,128)(2,1)S(1)} reshape(bf16[32,16,32,16]{3,2,1,0:T(8,128)(2,1)} %get-tuple-element.41) | data formatting | bytes 1048576 | tf_op jit(solution)/shard_map/convert_element_type | solution.py:208
  39.4 7.8 %convert_element_type.58.low_ref = bf16[512,512]{1,0:T(8,128)(2,1)S(1)} reshape(bf16[32,16,32,16]{3,2,1,0:T(8,128)(2,1)} %get-tuple-element.40) | data formatting | bytes 1048576 | tf_op jit(solution)/shard_map/convert_element_type | solution.py:208
  47.2 23.0 %all-to-all-done.1 = bf16[4,128,2048]{1,0,2:T(4,128)(2,1)} async-done(((bf16[4,128,2048]{1,0,2:T(4,128)(2,1)}), bf16[4,128,2048]{1,0,2:T(4,128)(2,1)}, u32[]{:S(2)}, u32[]{:S(2)}) %all-to-all-start.1) | async-done | bytes 2097184 | tf_op jit(solution)/shard_map/all_to_all | solution.py:177
  70.2 3.2 copy.71
  73.4 3.9 %copy.72 = bf16[8,4,128,256]{3,2,1,0:T(8,128)(2,1)} copy(bf16[8,4,128,256]{2,3,0,1:T(8,128)(2,1)} %bitcast.96) | data formatting | bytes 4194304 | tf_op jit(solution)/shard_map/all_to_all | solution.py:177
  79.0 3.8 %mix.2 = bf16[32,128,256]{2,1,0:T(8,128)(2,1)S(1)} custom-call(bf16[512,512]{1,0:T(8,128)(2,1)S(1)} %convert_element_type.56.high_ref, bf16[512,512]{1,0:T(8,128)(2,1)S(1)} %convert_element_type.58.low_ref, bf16[32,128,256]{2,1,0:T(8,128)(2,1)S(1)} %bitcast.91), custom_call_target="tpu_custom_call" | custom-call | tf_op jit(solution)/shard_map/mix/pallas_call | solution.py:53
  84.1 4.5 %all-to-all-start.2 = ((bf16[32,128,256]{2,1,0:T(8,128)(2,1)}), bf16[32,128,256]{2,1,0:T(8,128)(2,1)}, u32[]{:S(2)}, u32[]{:S(2)}) async-start(bf16[32,128,256]{2,1,0:T(8,128)(2,1)} %copy-done.2), calls=%async_computation.2 | async-start | bytes 4194304 | tf_op jit(solution)/shard_map/all_to_all | solution.py:178
  89.5 4.4 %collective-permute-start.2 = (bf16[16,2048]{1,0:T(8,128)(2,1)}, bf16[16,2048]{1,0:T(8,128)(2,1)}, u32[]{:S(2)}, u32[]{:S(2)}) collective-permute-start(bf16[16,2048]{1,0:T(8,128)(2,1)} %bitcast.82), channel_id=1, source_target_pairs={{0,1},{1,2},{2,3},{3,4},{4,5},{5,6},{6,7},{8,9},{9,10},{10,11},{11... | collective-permute-start | bytes 196616 | tf_op jit(solution)/shard_map/ppermute | solution.py:37
  97.1 1.7 copy.65
  101.2 13.2 %cholesky.51 = f32[128,128]{1,0:T(8,128)} custom-call(f32[128,128]{1,0:T(8,128)} %cholesky.124), custom_call_target="Cholesky" | custom-call | tf_op jit(solution)/shard_map/jit(cholesky)/cholesky | solution.py:216
  115.9 11.3 %custom-call.15 = f32[1,128,128]{1,2,0:T(8,128)} custom-call(f32[1,128,128]{2,1,0:T(8,128)} %get-tuple-element.35), custom_call_target="InvertDiagBlocksLowerTriangular" | custom-call | tf_op jit(solution)/shard_map/jit(cholesky)/cholesky | solution.py:216
  131.9 6.8 %cholesky.110 = f32[60,60]{1,0:T(8,128)} custom-call(f32[60,60]{1,0:T(8,128)} %convolution_subtract_fusion.1), custom_call_target="Cholesky" | custom-call | tf_op jit(solution)/shard_map/jit(cholesky)/cholesky | solution.py:216
  144.9 21.1 %custom-call.16 = f32[2,128,128]{1,2,0:T(8,128)} custom-call(f32[2,128,128]{2,1,0:T(8,128)} %pad_maximum_fusion), custom_call_target="InvertDiagBlocksLowerTriangular" | custom-call | tf_op jit(solution)/shard_map/jit(_solve_triangular)/triangular_solve | solution.py:217
  170.7 6.5 %primal.2.refs_0_ = f32[512,2048]{1,0:T(8,128)} custom-call(bf16[512,188]{1,0:T(8,128)(2,1)S(1)} %bitcast.92, bf16[188,2048]{1,0:T(8,128)(2,1)S(1)} %copy-done.1, f32[188,188]{1,0:T(8,128)S(1)} %fusion.inverse_ref, bf16[512,2048]{1,0:T(8,128)(2,1)S(1)} %bitcast.84), custom_call_target="tpu_custom_call" | custom-call | flops 1577058304 | bytes 12582912 | tf_op jit(solution)/shard_map/primal/pallas_call | solution.py:103
  177.9 2.8 copy.73
  181.4 9.2 %update.2 = (bf16[512,2048]{1,0:T(8,128)(2,1)S(1)}, f32[512,2048]{1,0:T(8,128)}) custom-call(f32[512,2048]{1,0:T(8,128)} %primal.2.refs_0_, bf16[512,2048]{1,0:T(8,128)(2,1)S(1)} %bitcast.88, bf16[16,32,2048]{2,1,0:T(8,128)(2,1)} %refs_2_.1, bf16[32,2048]{1,0:T(8,128)(2,1)S(1)} %collective-permute-done.refs_3_, ...), custom_call_target="tpu_custom_call" | custom-call | tf_op jit(solution)/shard_map/update/pallas_call | solution.py:165
  190.6 2.5 copy.76
  193.1 53.1 %all_to_all.71 = bf16[4,128,2048]{1,0,2:T(4,128)(2,1)S(1)} all-to-all(bf16[4,128,2048]{1,0,2:T(4,128)(2,1)} %copy.76), channel_id=1, replica_groups=mesh['row'=4,'col'=8] {'col'}, dimensions={2} | all-to-all | bytes 4194304 | tf_op jit(solution)/shard_map/all_to_all | solution.py:177
  247.9 4.0 %copy.78 = bf16[8,4,128,256]{3,2,1,0:T(8,128)(2,1)} copy(bf16[8,4,128,256]{2,3,0,1:T(8,128)(2,1)} %bitcast.98) | data formatting | bytes 4194304 | tf_op jit(solution)/shard_map/all_to_all | solution.py:177
  254.4 3.8 %mix.3 = bf16[32,128,256]{2,1,0:T(8,128)(2,1)S(1)} custom-call(bf16[512,512]{1,0:T(8,128)(2,1)S(1)} %convert_element_type.56.high_ref, bf16[512,512]{1,0:T(8,128)(2,1)S(1)} %copy-done.7, bf16[32,128,256]{2,1,0:T(8,128)(2,1)S(1)} %bitcast.90), custom_call_target="tpu_custom_call" | custom-call | tf_op jit(solution)/shard_map/mix/pallas_call | solution.py:53
  259.6 4.5 %all-to-all-start.4 = ((bf16[32,128,256]{2,1,0:T(8,128)(2,1)}), bf16[32,128,256]{2,1,0:T(8,128)(2,1)}, u32[]{:S(2)}, u32[]{:S(2)}) async-start(bf16[32,128,256]{2,1,0:T(8,128)(2,1)} %copy-done.3), calls=%async_computation.4 | async-start | bytes 4194304 | tf_op jit(solution)/shard_map/all_to_all | solution.py:178
  268.3 3.8 %collective-permute-start.6 = (bf16[16,2048]{1,0:T(8,128)(2,1)}, bf16[16,2048]{1,0:T(8,128)(2,1)S(1)}, u32[]{:S(2)}, u32[]{:S(2)}) collective-permute-start(bf16[16,2048]{1,0:T(8,128)(2,1)} %bitcast.80), channel_id=1, source_target_pairs={{0,1},{1,2},{2,3},{3,4},{4,5},{5,6},{6,7},{8,9},{9,10},{10,11},{11... | collective-permute-start | bytes 196616 | tf_op jit(solution)/shard_map/ppermute | solution.py:37
  274.1 8.3 %primal.3.refs_0_ = f32[512,2048]{1,0:T(8,128)} custom-call(bf16[512,188]{1,0:T(8,128)(2,1)S(1)} %bitcast.93, bf16[188,2048]{1,0:T(8,128)(2,1)S(1)} %copy-done.1, f32[188,188]{1,0:T(8,128)S(1)} %copy-done.11, bf16[512,2048]{1,0:T(8,128)(2,1)S(1)} %get-tuple-element.4.tile_ref, f32[512,2048]{1,0:T(8,128)} %get-tuple-element.5.rest_0_.refs_8_), custom_call_target="tpu_custom_call" | custom-call | flops 1577058304 | bytes 12582912 | tf_op jit(solution)/shard_map/primal/pallas_call | solution.py:103
  282.4 29.6 %all-to-all-done.4 = bf16[32,128,256]{2,1,0:T(8,128)(2,1)} async-done(((bf16[32,128,256]{2,1,0:T(8,128)(2,1)}), bf16[32,128,256]{2,1,0:T(8,128)(2,1)}, u32[]{:S(2)}, u32[]{:S(2)}) %all-to-all-start.4) | async-done | bytes 2097184 | tf_op jit(solution)/shard_map/all_to_all | solution.py:178
  312.0 2.8 copy.79
  315.5 9.4 %update.3 = bf16[512,2048]{1,0:T(8,128)(2,1)} custom-call(f32[512,2048]{1,0:T(8,128)} %primal.3.refs_0_, bf16[512,2048]{1,0:T(8,128)(2,1)S(1)} %bitcast.89, bf16[16,32,2048]{2,1,0:T(8,128)(2,1)S(1)} %bitcast.87, bf16[32,2048]{1,0:T(8,128)(2,1)S(1)} %collective-permute-done.4.refs_3_, bf16[32,2048]{1,0:T(8,128)(2,1)} %collective-permute-done.5.refs_4_, ...), custom_call_target="tpu_custom_call" | custom-call | tf_op jit(solution)/shard_map/update/pallas_call | solution.py:165
  324.9 2.3 fusion.24
  (96 shorter events, 48.5 us)
Async XLA Ops:
  4.8 13.6 %all-to-all-start = ((f32[8,1,128]{2,1,0:T(1,128)}), f32[8,1,128]{2,1,0:T(1,128)S(1)}, u32[]{:S(2)}, u32[]{:S(2)}) async-start(f32[8,1,128]{2,1,0:T(1,128)} %reshape.205), calls=%async_computation | async-start | bytes 8192 | tf_op jit(solution)/shard_map/all_to_all | solution.py:198
  16.3 6.5 %copy-start = (bf16[16,32,2048]{2,1,0:T(8,128)(2,1)S(1)}, bf16[16,32,2048]{2,1,0:T(8,128)(2,1)}, u32[]{:S(2)}) copy-start(bf16[16,32,2048]{2,1,0:T(8,128)(2,1)} %refs_2_.1) | copy-start | bytes 6291460
  18.5 51.8 %all-to-all-start.1 = ((bf16[4,128,2048]{1,0,2:T(4,128)(2,1)}), bf16[4,128,2048]{1,0,2:T(4,128)(2,1)}, u32[]{:S(2)}, u32[]{:S(2)}) async-start(bf16[4,128,2048]{1,0,2:T(4,128)(2,1)} %copy.70), calls=%async_computation.1 | async-start | bytes 4194304 | tf_op jit(solution)/shard_map/all_to_all | solution.py:177
  23.6 157.8 %collective-permute-start = (bf16[32,2048]{1,0:T(8,128)(2,1)}, bf16[32,2048]{1,0:T(8,128)(2,1)S(1)}, u32[]{:S(2)}, u32[]{:S(2)}) collective-permute-start(bf16[32,2048]{1,0:T(8,128)(2,1)} %get-tuple-element.33), channel_id=1, source_target_pairs={{0,8},{8,16},{16,24},{1,9},{9,17},{17,25},{2,10},{10,18},{18,26},{... | collective-permute-start | bytes 393224 | tf_op jit(solution)/shard_map/ppermute | solution.py:37
  24.8 156.5 %collective-permute-start.1 = (bf16[32,2048]{1,0:T(8,128)(2,1)}, bf16[32,2048]{1,0:T(8,128)(2,1)}, u32[]{:S(2)}, u32[]{:S(2)}) collective-permute-start(bf16[32,2048]{1,0:T(8,128)(2,1)} %get-tuple-element.32), channel_id=1, source_target_pairs={{8,0},{16,8},{24,16},{9,1},{17,9},{25,17},{10,2},{18,10},{26,18},{... | collective-permute-start | bytes 393224 | tf_op jit(solution)/shard_map/ppermute | solution.py:37
  47.2 30.1 %copy-start.6 = (bf16[512,512]{1,0:T(8,128)(2,1)}, bf16[512,512]{1,0:T(8,128)(2,1)S(1)}, u32[]{:S(2)}) copy-start(bf16[512,512]{1,0:T(8,128)(2,1)S(1)} %convert_element_type.58.low_ref) | copy-start | bytes 1572868
  77.4 1.6 copy-start.5
  82.8 1.3 copy-start.2
  84.1 11.9 %copy-start.1 = (bf16[188,2048]{1,0:T(8,128)(2,1)S(1)}, bf16[188,2048]{1,0:T(8,128)(2,1)}, u32[]{:S(2)}) copy-start(bf16[188,2048]{1,0:T(8,128)(2,1)} %library_ref.3) | copy-start | bytes 2310148
  84.1 93.8 %all-to-all-start.2 = ((bf16[32,128,256]{2,1,0:T(8,128)(2,1)}), bf16[32,128,256]{2,1,0:T(8,128)(2,1)}, u32[]{:S(2)}, u32[]{:S(2)}) async-start(bf16[32,128,256]{2,1,0:T(8,128)(2,1)} %copy-done.2), calls=%async_computation.2 | async-start | bytes 4194304 | tf_op jit(solution)/shard_map/all_to_all | solution.py:178
  89.5 91.9 %collective-permute-start.2 = (bf16[16,2048]{1,0:T(8,128)(2,1)}, bf16[16,2048]{1,0:T(8,128)(2,1)}, u32[]{:S(2)}, u32[]{:S(2)}) collective-permute-start(bf16[16,2048]{1,0:T(8,128)(2,1)} %bitcast.82), channel_id=1, source_target_pairs={{0,1},{1,2},{2,3},{3,4},{4,5},{5,6},{6,7},{8,9},{9,10},{10,11},{11... | collective-permute-start | bytes 196616 | tf_op jit(solution)/shard_map/ppermute | solution.py:37
  94.6 86.8 %collective-permute-start.3 = (bf16[16,2048]{1,0:T(8,128)(2,1)}, bf16[16,2048]{1,0:T(8,128)(2,1)}, u32[]{:S(2)}, u32[]{:S(2)}) collective-permute-start(bf16[16,2048]{1,0:T(8,128)(2,1)} %bitcast.81), channel_id=1, source_target_pairs={{1,0},{2,1},{3,2},{4,3},{5,4},{6,5},{7,6},{9,8},{10,9},{11,10},{12... | collective-permute-start | bytes 196616 | tf_op jit(solution)/shard_map/ppermute | solution.py:37
  99.9 0.7 copy-start.14
  143.5 0.7 copy-start.13
  169.7 1.0 copy-start.8
  177.2 0.7 copy-start.10
  180.7 0.7 copy-start.12
  251.8 1.6 copy-start.4
  253.4 1.0 copy-start.7
  258.3 1.3 copy-start.3
  259.6 14.5 %copy-start.9 = (bf16[16,32,188]{2,1,0:T(8,128)(2,1)S(1)}, bf16[16,32,188]{2,1,0:T(8,128)(2,1)}, u32[]{:S(2)}) copy-start(bf16[16,32,188]{2,1,0:T(8,128)(2,1)} %param.9) | copy-start | bytes 577540
  259.6 14.5 %copy-start.11 = (f32[188,188]{1,0:T(8,128)S(1)}, f32[188,188]{1,0:T(8,128)}, u32[]{:S(2)}) copy-start(f32[188,188]{1,0:T(8,128)} %copy-done.10) | copy-start | bytes 424132
  259.6 52.4 %all-to-all-start.4 = ((bf16[32,128,256]{2,1,0:T(8,128)(2,1)}), bf16[32,128,256]{2,1,0:T(8,128)(2,1)}, u32[]{:S(2)}, u32[]{:S(2)}) async-start(bf16[32,128,256]{2,1,0:T(8,128)(2,1)} %copy-done.3), calls=%async_computation.4 | async-start | bytes 4194304 | tf_op jit(solution)/shard_map/all_to_all | solution.py:178
  264.8 50.6 %collective-permute-start.4 = (bf16[32,2048]{1,0:T(8,128)(2,1)}, bf16[32,2048]{1,0:T(8,128)(2,1)S(1)}, u32[]{:S(2)}, u32[]{:S(2)}) collective-permute-start(bf16[32,2048]{1,0:T(8,128)(2,1)} %get-tuple-element.29), channel_id=1, source_target_pairs={{0,8},{8,16},{16,24},{1,9},{9,17},{17,25},{2,10},{10,18},{18,26},{... | collective-permute-start | bytes 393224 | tf_op jit(solution)/shard_map/ppermute | solution.py:37
  266.1 49.4 %collective-permute-start.5 = (bf16[32,2048]{1,0:T(8,128)(2,1)}, bf16[32,2048]{1,0:T(8,128)(2,1)}, u32[]{:S(2)}, u32[]{:S(2)}) collective-permute-start(bf16[32,2048]{1,0:T(8,128)(2,1)} %get-tuple-element.28), channel_id=1, source_target_pairs={{8,0},{16,8},{24,16},{9,1},{17,9},{25,17},{10,2},{18,10},{26,18},{... | collective-permute-start | bytes 393224 | tf_op jit(solution)/shard_map/ppermute | solution.py:37
  268.3 47.1 %collective-permute-start.6 = (bf16[16,2048]{1,0:T(8,128)(2,1)}, bf16[16,2048]{1,0:T(8,128)(2,1)S(1)}, u32[]{:S(2)}, u32[]{:S(2)}) collective-permute-start(bf16[16,2048]{1,0:T(8,128)(2,1)} %bitcast.80), channel_id=1, source_target_pairs={{0,1},{1,2},{2,3},{3,4},{4,5},{5,6},{6,7},{8,9},{9,10},{10,11},{11... | collective-permute-start | bytes 196616 | tf_op jit(solution)/shard_map/ppermute | solution.py:37
  272.8 42.7 %collective-permute-start.7 = (bf16[16,2048]{1,0:T(8,128)(2,1)}, bf16[16,2048]{1,0:T(8,128)(2,1)}, u32[]{:S(2)}, u32[]{:S(2)}) collective-permute-start(bf16[16,2048]{1,0:T(8,128)(2,1)} %bitcast.79), channel_id=1, source_target_pairs={{1,0},{2,1},{3,2},{4,3},{5,4},{6,5},{7,6},{9,8},{10,9},{11,10},{12... | collective-permute-start | bytes 196616 | tf_op jit(solution)/shard_map/ppermute | solution.py:37

commit v3 on v2

--- a/solution.py
+++ b/solution.py
@@ -35,6 +35,36 @@
     last = lax.index_in_dim(tile, tile.shape[dim] - 1, dim, keepdims=False)
     first = lax.index_in_dim(tile, 0, dim, keepdims=False)
     return lax.ppermute(last, axis, forward), lax.ppermute(first, axis, backward)
+
+
+def spread_kernel(weights_ref, high_ref, low_ref):
+    weights = weights_ref[...]
+    count = weights.shape[0]
+    side = count * GROUP
+    high = weights.astype(jnp.bfloat16)
+    low = (weights - high.astype(jnp.float32)).astype(jnp.bfloat16)
+    owner = lax.broadcasted_iota(jnp.int32, (side, count), 0) // GROUP
+    expand = (owner == lax.broadcasted_iota(jnp.int32, (side, count), 1)).astype(jnp.float32)
+    expand = expand.astype(jnp.bfloat16)
+    rows = lax.broadcasted_iota(jnp.int32, (side, side), 0) % GROUP
+    same = rows == lax.broadcasted_iota(jnp.int32, (side, side), 1) % GROUP
+    for part, out_ref in ((high, high_ref), (low, low_ref)):
+        tall = jnp.dot(expand, part, preferred_element_type=jnp.float32).astype(jnp.bfloat16)
+        full = lax.dot_general(
+            tall, expand, (((1,), (1,)), ((), ())), preferred_element_type=jnp.float32
+        )
+        out_ref[...] = jnp.where(same, full, 0.0).astype(jnp.bfloat16)
+
+
+def spread(weights):
+    side = weights.shape[0] * GROUP
+    shape = jax.ShapeDtypeStruct((side, side), jnp.bfloat16)
+    return pl.pallas_call(
+        spread_kernel,
+        out_shape=[shape, shape],
+        compiler_params=pltpu.CompilerParams(vmem_limit_bytes=VMEM),
+        name="spread",
+    )(weights)
 
 
 def mix_kernel(high_ref, low_ref, strip_ref, out_ref):
@@ -121,7 +151,7 @@
     refs = refs[8:]
     dual_ref = refs[0] if has_dual else None
     fresh_ref = refs[1 if has_dual else 0]
-    new_ref = refs[-1] if keep_dual else None
+    new_ref, strip_ref = refs[-2:] if keep_dual else (None, None)
     rows, columns, atoms = tile_ref.shape
     threshold = threshold_ref[...]
     left = left_ref[...].astype(jnp.float32)
@@ -138,21 +168,24 @@
         pixels = pl.ds(row * columns, columns)
         primal = primal_ref[pixels]
         base = primal - dual_ref[pixels] if has_dual else primal
-        averaged = jnp.sqrt(jnp.sqrt(averaged_ref[pixels].astype(jnp.float32)))
+        averaged = jnp.sqrt(jnp.sqrt(averaged_ref[0, pixels].astype(jnp.float32)))
         blend = (base + GAMMA * averaged + ETA * spatial) / (1.0 + GAMMA + ETA)
         fresh = jnp.maximum(blend - threshold, 0.0)
-        fresh_ref[pixels] = fresh.astype(jnp.bfloat16)
+        rounded = fresh.astype(jnp.bfloat16)
+        fresh_ref[pixels] = rounded
         if keep_dual:
             new_ref[pixels] = fresh - base
+            strip_ref[0, pixels] = rounded
         above, here = here, below
 
 
 def update(primal, averaged, tile, halo, threshold, dual, keep_dual):
     rows, columns, atoms = tile.shape
     pixels = rows * columns
-    width = min(256, atoms)
+    width = averaged.shape[2]
+    strip = pl.BlockSpec((1, pixels, width), lambda i: (i, 0, 0))
     flat = pl.BlockSpec((pixels, width), lambda i: (0, i))
-    specs = [flat, flat, pl.BlockSpec((rows, columns, width), lambda i: (0, 0, i))]
+    specs = [flat, strip, pl.BlockSpec((rows, columns, width), lambda i: (0, 0, i))]
     specs += [pl.BlockSpec((part.shape[0], width), lambda i: (0, i)) for part in halo]
     specs += [pl.BlockSpec((1, width), lambda i: (0, i))]
     arrays = [primal, averaged, tile, *halo, threshold.reshape(1, -1)]
@@ -162,20 +195,21 @@
     shapes = [jax.ShapeDtypeStruct((pixels, atoms), jnp.bfloat16)]
     if keep_dual:
         shapes.append(jax.ShapeDtypeStruct((pixels, atoms), jnp.float32))
+        shapes.append(jax.ShapeDtypeStruct(averaged.shape, jnp.bfloat16))
     return pl.pallas_call(
         functools.partial(update_kernel, dual is not None, keep_dual),
         out_shape=shapes,
         grid=(atoms // width,),
         in_specs=specs,
-        out_specs=[flat] * len(shapes),
+        out_specs=[flat, flat, strip] if keep_dual else [flat],
         compiler_params=pltpu.CompilerParams(vmem_limit_bytes=VMEM),
         name="update",
     )(*arrays)
 
 
-def exchange(tiles, high, low):
-    strip = lax.all_to_all(tiles, "col", split_axis=2, concat_axis=0, tiled=True)
-    return lax.all_to_all(mix(high, low, strip), "col", split_axis=0, concat_axis=2, tiled=True)
+def cut(tile, group):
+    pixels, atoms = tile.shape
+    return tile.reshape(pixels, group, atoms // group).transpose(1, 0, 2)
 
 
 def local(
@@ -197,47 +231,41 @@
     parts = jnp.broadcast_to(part, (group,) + part.shape[1:])
     weights = lax.all_to_all(parts, "col", split_axis=0, concat_axis=0, tiled=True)
     weights = weights.reshape(group * blocks, group * blocks)
-    high = lax.reduce_precision(weights, 8, 7)
-    low = weights - high
-    eye = jnp.eye(GROUP, dtype=jnp.float32)
-
-    def spread(matrix):
-        side = matrix.shape[0] * GROUP
-        return (
-            (matrix[:, None, :, None] * eye[None, :, None, :]).reshape(side, side)
-        ).astype(jnp.bfloat16)
-
-    high, low = spread(high), spread(low)
+    high, low = spread(weights)
 
     bands = library.shape[0]
     gram = jnp.dot(library, library.T, preferred_element_type=jnp.float32) + MU * jnp.eye(
         bands, dtype=jnp.float32
     )
     chol = jnp.linalg.cholesky(gram)
-    half = jax.scipy.linalg.solve_triangular(chol, jnp.eye(bands, dtype=jnp.float32), lower=True)
-    inverse = lax.dot_general(
-        half, half, (((0,), (0,)), ((), ())), precision=lax.Precision.HIGHEST
-    )
     seen = observed.reshape(pixels, -1)
     dual = None
     current = warm
+    strips = cut(warm.reshape(pixels, atoms), group)
     for step in range(ITERS):
-        averaged = exchange(current.reshape(blocks, block_pixels, atoms), high, low)
+        strip = lax.all_to_all(strips, "col", split_axis=0, concat_axis=0, tiled=True)
+        if step == 0:
+            strip, chol = lax.optimization_barrier((strip, chol))
+            half = jax.scipy.linalg.solve_triangular(
+                chol, jnp.eye(bands, dtype=jnp.float32), lower=True
+            )
+            inverse = lax.dot_general(
+                half, half, (((0,), (0,)), ((), ())), precision=lax.Precision.HIGHEST
+            )
+        sums = mix(high, low, strip.reshape(group * blocks, block_pixels, -1))
+        averaged = lax.all_to_all(
+            sums.reshape(strips.shape), "col", split_axis=0, concat_axis=0, tiled=True
+        )
         top, bottom = beside(current, "row", 0)
         left, right = beside(current, "col", 1)
         flat = current.reshape(pixels, atoms)
         primal = primal_step(seen, library, inverse, flat, dual)
         keep = step + 1 < ITERS
         out = update(
-            primal,
-            averaged.reshape(pixels, atoms),
-            current,
-            (top, bottom, left, right),
-            threshold,
-            dual,
-            keep,
+            primal, averaged, current, (top, bottom, left, right), threshold, dual, keep
         )
-        dual = out[1] if keep else None
+        if keep:
+            dual, strips = out[1:]
         current = out[0].reshape(tile_rows, tile_cols, atoms)
     rebuilt = jnp.dot(current.reshape(pixels, atoms), library.T, preferred_element_type=jnp.float32)
     misfit = observed.astype(jnp.float32) - rebuilt.reshape(tile_rows, tile_cols, -1)

time: 331 us -> 264 us (0.80)
  local copies, waits for them, and re-layouts: 61.8 us -> 16.5 us
  other arithmetic: 68.3 us -> 56.4 us
  waiting for transfers between devices: 54.8 us -> 48 us
  matrix products: 10.2 us -> 5.97 us
    all_to_all x6 -> x0, local copies, waits for them, and re-layouts: 18.2 us -> none  [the longest x4 12.7 us: exchange(): lax.all_to_all(tiles, 'col', split_axis=2, concat_axis=0, tiled=True)]
    convert_element_type x2 -> x0, local copies, waits for them, and re-layouts: 15.6 us -> none  [spread(): return (matrix[:, None, :, None] * eye[None, :, None, :]).reshape(side, s...]
    all_to_all x3, waiting for transfers between devices: 52.6 us -> 44.2 us  [the longest x2 30.7 us: local(): lax.all_to_all(sums.reshape(strips.shape), 'col', split_axis=0, concat_ax...]
    another operation x7, other arithmetic: 35.4 us -> 28.4 us  [local(): chol = jnp.linalg.cholesky(gram)]
    convert_element_type x2 -> x0, other arithmetic: 4.25 us -> none  [the longest x1 4.24 us: spread(): return (matrix[:, None, :, None] * eye[None, :, None, :]).reshape(side, s...]
    reshape x1 -> x0, local copies, waits for them, and re-layouts: 4.24 us -> none  [local(): averaged = exchange(current.reshape(blocks, block_pixels, atoms), high, low)]
    ppermute x4, starting transfers between devices: 10.8 us -> 14.3 us  [beside(): lax.ppermute(last, axis, forward)]
    unnamed x38 -> x41, local copies, waits for them, and re-layouts: 14.6 us -> 12.6 us
  transfers between devices with their start and end apart: 12 -> 12, of which waited for: 3 -> 5; matrix products, arithmetic and copies ran while one was open for 35% -> 24% of each run, Pallas kernels for 6% -> 6%
where the time goes in v3:
time: 264 us; the launch traced here: 263 us
  other arithmetic  56.4 us (21%)
  blocking collectives  52.1 us (20%)
  waiting for transfers between devices  48 us (18%)
  Pallas kernels  41.9 us (16%)
  starting transfers between devices  39.5 us (15%)
  local copies, waits for them, and re-layouts  16.5 us (6%)
  matrix products  5.97 us (2%)
    all_to_all x1, blocking collectives, local(): lax.all_to_all(strips, 'col', split_axis=0, concat_axis=0, tiled=True)  52.1 us
    all_to_all x2, waiting for transfers between devices, local(): lax.all_to_all(sums.reshape(strips.shape), 'col', split_axis=0, concat_ax...  30.7 us
    another operation x7, other arithmetic, local(): chol = jnp.linalg.cholesky(gram)  28.4 us
    another operation x6, other arithmetic, local(): jax.scipy.linalg.solve_triangular(chol, jnp.eye(bands, dtype=jnp.float32)...  21.3 us
    pallas_call x2, Pallas kernels, update(): pl.pallas_call(functools.partial(update_kernel, dual is not None, keep_du...  19 us
    pallas_call x2, Pallas kernels, primal_step(): pl.pallas_call(primal_kernel, out_shape=jax.ShapeDtypeStruct((pixels, ato...  14.6 us
    ppermute x4, starting transfers between devices, beside(): lax.ppermute(last, axis, forward)  14.3 us
    all_to_all x1, waiting for transfers between devices, local(): lax.all_to_all(strips, 'col', split_axis=0, concat_axis=0, tiled=True)  13.5 us
  transfers between devices with their start and end apart: 12, of which 5 were waited for; matrix products, arithmetic and copies ran while one was open for 24% of the time, Pallas kernels for 6%

profile of v3, /device:TPU:0, one launch (start us, length us, event | category | flops | bytes accessed | tf_op | source)
XLA Modules:
  0.0 262.8 jit_solution(12835839392894256695)
XLA Ops:
  4.8 7.3 %all-to-all-start.1 = ((f32[8,1,128]{2,1,0:T(1,128)}), f32[8,1,128]{2,1,0:T(1,128)S(1)}, u32[]{:S(2)}, u32[]{:S(2)}) async-start(f32[8,1,128]{2,1,0:T(1,128)} %reshape.177), calls=%async_computation.1 | async-start | bytes 8192 | tf_op jit(solution)/shard_map/all_to_all | solution.py:232
  12.1 2.3 copy.45
  14.4 1.7 copy.51
  16.1 2.4 all-to-all-done.1
  18.5 3.8 %all-to-all-start = ((bf16[8,512,256]{2,1,0:T(8,128)(2,1)}), bf16[8,512,256]{2,1,0:T(8,128)(2,1)S(1)}, u32[]{:S(2)}, u32[]{:S(2)}) async-start(bf16[8,512,256]{2,1,0:T(8,128)(2,1)} %bitcast.82), calls=%async_computation | async-start | bytes 4194304 | tf_op jit(solution)/shard_map/all_to_all | solution.py:246
  22.8 11.7 %cholesky.51 = f32[128,128]{1,0:T(8,128)S(1)} custom-call(f32[128,128]{1,0:T(8,128)S(1)} %cholesky.124), custom_call_target="Cholesky" | custom-call | tf_op jit(solution)/shard_map/jit(cholesky)/cholesky | solution.py:240
  34.6 9.8 %custom-call.15 = f32[1,128,128]{1,2,0:T(8,128)S(1)} custom-call(f32[1,128,128]{2,1,0:T(8,128)S(1)} %get-tuple-element.45), custom_call_target="InvertDiagBlocksLowerTriangular" | custom-call | tf_op jit(solution)/shard_map/jit(cholesky)/cholesky | solution.py:240
  44.8 5.5 %cholesky.110 = f32[60,60]{1,0:T(8,128)S(1)} custom-call(f32[60,60]{1,0:T(8,128)S(1)} %convolution_subtract_fusion.1), custom_call_target="Cholesky" | custom-call | tf_op jit(solution)/shard_map/jit(cholesky)/cholesky | solution.py:240
  56.4 13.5 %all-to-all-done = bf16[8,512,256]{2,1,0:T(8,128)(2,1)S(1)} async-done(((bf16[8,512,256]{2,1,0:T(8,128)(2,1)}), bf16[8,512,256]{2,1,0:T(8,128)(2,1)S(1)}, u32[]{:S(2)}, u32[]{:S(2)}) %all-to-all-start) | async-done | bytes 2097184 | tf_op jit(solution)/shard_map/all_to_all | solution.py:246
  70.9 3.8 %mix.2 = bf16[32,128,256]{2,1,0:T(8,128)(2,1)S(1)} custom-call(bf16[512,512]{1,0:T(8,128)(2,1)S(1)} %get-tuple-element.10.high_ref, bf16[512,512]{1,0:T(8,128)(2,1)S(1)} %copy-done.8, bf16[32,128,256]{2,1,0:T(8,128)(2,1)S(1)} %bitcast.74), custom_call_target="tpu_custom_call" | custom-call | tf_op jit(solution)/shard_map/mix/pallas_call | solution.py:83
  74.8 1.3 copy-done.2
  76.1 4.5 %all-to-all-start.2 = ((bf16[8,512,256]{2,1,0:T(8,128)(2,1)}), bf16[8,512,256]{2,1,0:T(8,128)(2,1)}, u32[]{:S(2)}, u32[]{:S(2)}) async-start(bf16[8,512,256]{2,1,0:T(8,128)(2,1)} %bitcast.73), calls=%async_computation.2 | async-start | bytes 4194304 | tf_op jit(solution)/shard_map/all_to_all | solution.py:256
  82.6 3.7 %collective-permute-start = (bf16[32,2048]{1,0:T(8,128)(2,1)}, bf16[32,2048]{1,0:T(8,128)(2,1)}, u32[]{:S(2)}, u32[]{:S(2)}) collective-permute-start(bf16[32,2048]{1,0:T(8,128)(2,1)} %get-tuple-element.43), channel_id=1, source_target_pairs={{0,8},{8,16},{16,24},{1,9},{9,17},{17,25},{2,10},{10,18},{18,26},{... | collective-permute-start | bytes 393224 | tf_op jit(solution)/shard_map/ppermute | solution.py:37
  87.2 3.8 %collective-permute-start.2 = (bf16[16,2048]{1,0:T(8,128)(2,1)}, bf16[16,2048]{1,0:T(8,128)(2,1)S(1)}, u32[]{:S(2)}, u32[]{:S(2)}) collective-permute-start(bf16[16,2048]{1,0:T(8,128)(2,1)} %bitcast.68), channel_id=1, source_target_pairs={{0,1},{1,2},{2,3},{3,4},{4,5},{5,6},{6,7},{8,9},{9,10},{10,11},{11... | collective-permute-start | bytes 196616 | tf_op jit(solution)/shard_map/ppermute | solution.py:37
  91.6 1.5 collective-permute-start.3
  95.9 20.5 %custom-call.16 = f32[2,128,128]{1,2,0:T(8,128)S(1)} custom-call(f32[2,128,128]{2,1,0:T(8,128)} %pad_maximum_fusion), custom_call_target="InvertDiagBlocksLowerTriangular" | custom-call | tf_op jit(solution)/shard_map/jit(_solve_triangular)/triangular_solve | solution.py:249
  119.3 6.5 %primal.2.refs_0_ = f32[512,2048]{1,0:T(8,128)} custom-call(bf16[512,188]{1,0:T(8,128)(2,1)S(1)} %bitcast.77, bf16[188,2048]{1,0:T(8,128)(2,1)S(1)} %copy-done.1, f32[188,188]{1,0:T(8,128)S(1)} %fusion.inverse_ref, bf16[512,2048]{1,0:T(8,128)(2,1)S(1)} %bitcast.70), custom_call_target="tpu_custom_call" | custom-call | flops 1577058304 | bytes 12582912 | tf_op jit(solution)/shard_map/primal/pallas_call | solution.py:133
  125.9 3.2 %all-to-all-done.2.refs_1_ = bf16[8,512,256]{2,1,0:T(8,128)(2,1)} async-done(((bf16[8,512,256]{2,1,0:T(8,128)(2,1)}), bf16[8,512,256]{2,1,0:T(8,128)(2,1)}, u32[]{:S(2)}, u32[]{:S(2)}) %all-to-all-start.2) | async-done | bytes 2097184 | tf_op jit(solution)/shard_map/all_to_all | solution.py:256
  129.1 9.5 %update.2 = (bf16[512,2048]{1,0:T(8,128)(2,1)S(1)}, f32[512,2048]{1,0:T(8,128)}, bf16[8,512,256]{2,1,0:T(8,128)(2,1)S(1)}) custom-call(f32[512,2048]{1,0:T(8,128)} %primal.2.refs_0_, bf16[8,512,256]{2,1,0:T(8,128)(2,1)} %all-to-all-done.2.refs_1_, bf16[16,32,2048]{2,1,0:T(8,128)(2,1)} %refs_2_.1, bf16[32,2048]{1,0:T(8,128)(2,1)} %collective-permute-done.refs_3_, ...), custom_call_target="tpu_custom_call" | custom-call | tf_op jit(solution)/shard_map/update/pallas_call | solution.py:199
  138.6 52.1 %all_to_all.25 = bf16[8,512,256]{2,1,0:T(8,128)(2,1)S(1)} all-to-all(bf16[8,512,256]{2,1,0:T(8,128)(2,1)S(1)} %get-tuple-element.15), channel_id=1, replica_groups=mesh['row'=4,'col'=8] {'col'}, dimensions={0} | all-to-all | bytes 4194304 | tf_op jit(solution)/shard_map/all_to_all | solution.py:246
  190.8 3.8 %mix.3 = bf16[32,128,256]{2,1,0:T(8,128)(2,1)S(1)} custom-call(bf16[512,512]{1,0:T(8,128)(2,1)S(1)} %copy-done.6, bf16[512,512]{1,0:T(8,128)(2,1)S(1)} %copy-done.9, bf16[32,128,256]{2,1,0:T(8,128)(2,1)S(1)} %bitcast.76), custom_call_target="tpu_custom_call" | custom-call | tf_op jit(solution)/shard_map/mix/pallas_call | solution.py:83
  194.6 1.3 copy-done.3
  195.9 4.4 %all-to-all-start.4 = ((bf16[8,512,256]{2,1,0:T(8,128)(2,1)}), bf16[8,512,256]{2,1,0:T(8,128)(2,1)}, u32[]{:S(2)}, u32[]{:S(2)}) async-start(bf16[8,512,256]{2,1,0:T(8,128)(2,1)} %bitcast.75), calls=%async_computation.4 | async-start | bytes 4194304 | tf_op jit(solution)/shard_map/all_to_all | solution.py:256
  200.6 3.8 %collective-permute-start.6 = (bf16[16,2048]{1,0:T(8,128)(2,1)S(1)}, bf16[16,2048]{1,0:T(8,128)(2,1)S(1)}, u32[]{:S(2)}, u32[]{:S(2)}) collective-permute-start(bf16[16,2048]{1,0:T(8,128)(2,1)S(1)} %bitcast.87), channel_id=1, source_target_pairs={{0,1},{1,2},{2,3},{3,4},{4,5},{5,6},{6,7},{8,9},{9,10},{10,11},{11... | collective-permute-start | bytes 196616 | tf_op jit(solution)/shard_map/ppermute | solution.py:37
  204.4 1.3 collective-permute-start.7
  205.7 1.3 collective-permute-start.5
  207.0 3.0 %collective-permute-start.4 = (bf16[32,2048]{1,0:T(8,128)(2,1)S(1)}, bf16[32,2048]{1,0:T(8,128)(2,1)S(1)}, u32[]{:S(2)}, u32[]{:S(2)}) collective-permute-start(bf16[32,2048]{1,0:T(8,128)(2,1)S(1)} %get-tuple-element.39), channel_id=1, source_target_pairs={{0,8},{8,16},{16,24},{1,9},{9,17},{17,25},{2,10},{10,18},{18,26},{... | collective-permute-start | bytes 393224 | tf_op jit(solution)/shard_map/ppermute | solution.py:37
  210.1 8.0 %primal.3.refs_0_ = f32[512,2048]{1,0:T(8,128)} custom-call(bf16[512,188]{1,0:T(8,128)(2,1)S(1)} %bitcast.78, bf16[188,2048]{1,0:T(8,128)(2,1)S(1)} %copy-done.1, f32[188,188]{1,0:T(8,128)S(1)} %fusion.inverse_ref, bf16[512,2048]{1,0:T(8,128)(2,1)S(1)} %get-tuple-element.13.tile_ref, f32[512,2048]{1,0:T(8,128)} %get-tuple-element.14.rest_0_.refs_8_), custom_call_target="tpu_custom_call" | custom-call | flops 1577058304 | bytes 12582912 | tf_op jit(solution)/shard_map/primal/pallas_call | solution.py:133
  218.1 1.5 collective-permute-done.6.refs_5_
  220.9 27.4 %all-to-all-done.4.refs_1_ = bf16[8,512,256]{2,1,0:T(8,128)(2,1)} async-done(((bf16[8,512,256]{2,1,0:T(8,128)(2,1)}), bf16[8,512,256]{2,1,0:T(8,128)(2,1)}, u32[]{:S(2)}, u32[]{:S(2)}) %all-to-all-start.4) | async-done | bytes 2097184 | tf_op jit(solution)/shard_map/all_to_all | solution.py:256
  250.1 9.5 %update.3 = bf16[512,2048]{1,0:T(8,128)(2,1)} custom-call(f32[512,2048]{1,0:T(8,128)} %primal.3.refs_0_, bf16[8,512,256]{2,1,0:T(8,128)(2,1)} %all-to-all-done.4.refs_1_, bf16[16,32,2048]{2,1,0:T(8,128)(2,1)S(1)} %bitcast.72, bf16[32,2048]{1,0:T(8,128)(2,1)S(1)} %copy-done.11, bf16[32,2048]{1,0:T(8,128)(2,1)S(1)} %collective-permute-done.5.refs_4_, ...), custom_call_target="tpu_custom_call" | custom-call | tf_op jit(solution)/shard_map/update/pallas_call | solution.py:199
  259.6 2.3 fusion.24
  (89 shorter events, 24.4 us)
Async XLA Ops:
  4.8 13.6 %all-to-all-start.1 = ((f32[8,1,128]{2,1,0:T(1,128)}), f32[8,1,128]{2,1,0:T(1,128)S(1)}, u32[]{:S(2)}, u32[]{:S(2)}) async-start(f32[8,1,128]{2,1,0:T(1,128)} %reshape.177), calls=%async_computation.1 | async-start | bytes 8192 | tf_op jit(solution)/shard_map/all_to_all | solution.py:232
  18.5 3.8 %copy-start.1 = (bf16[188,2048]{1,0:T(8,128)(2,1)S(1)}, bf16[188,2048]{1,0:T(8,128)(2,1)}, u32[]{:S(2)}) copy-start(bf16[188,2048]{1,0:T(8,128)(2,1)} %library_ref.3) | copy-start | bytes 2310148
  18.5 51.4 %all-to-all-start = ((bf16[8,512,256]{2,1,0:T(8,128)(2,1)}), bf16[8,512,256]{2,1,0:T(8,128)(2,1)S(1)}, u32[]{:S(2)}, u32[]{:S(2)}) async-start(bf16[8,512,256]{2,1,0:T(8,128)(2,1)} %bitcast.82), calls=%async_computation | async-start | bytes 4194304 | tf_op jit(solution)/shard_map/all_to_all | solution.py:246
  55.6 0.8 copy-start.7
  56.4 18.4 %copy-start.5 = (bf16[512,512]{1,0:T(8,128)(2,1)}, bf16[512,512]{1,0:T(8,128)(2,1)S(1)}, u32[]{:S(2)}) copy-start(bf16[512,512]{1,0:T(8,128)(2,1)S(1)} %get-tuple-element.10.high_ref) | copy-start | bytes 1572868
  69.9 1.0 copy-start.8
  74.8 1.3 copy-start.2
  76.1 4.5 %copy-start = (bf16[16,32,2048]{2,1,0:T(8,128)(2,1)S(1)}, bf16[16,32,2048]{2,1,0:T(8,128)(2,1)}, u32[]{:S(2)}) copy-start(bf16[16,32,2048]{2,1,0:T(8,128)(2,1)} %refs_2_.1) | copy-start | bytes 6291460
  76.1 18.3 %copy-start.15 = (f32[188,188]{1,0:T(8,128)S(1)}, f32[188,188]{1,0:T(8,128)}, u32[]{:S(2)}) copy-start(f32[188,188]{1,0:T(8,128)} %select_select_fusion) | copy-start | bytes 424132
  76.1 53.0 %all-to-all-start.2 = ((bf16[8,512,256]{2,1,0:T(8,128)(2,1)}), bf16[8,512,256]{2,1,0:T(8,128)(2,1)}, u32[]{:S(2)}, u32[]{:S(2)}) async-start(bf16[8,512,256]{2,1,0:T(8,128)(2,1)} %bitcast.73), calls=%async_computation.2 | async-start | bytes 4194304 | tf_op jit(solution)/shard_map/all_to_all | solution.py:256
  80.6 38.7 %copy-start.4 = (bf16[16,32,188]{2,1,0:T(8,128)(2,1)S(1)}, bf16[16,32,188]{2,1,0:T(8,128)(2,1)}, u32[]{:S(2)}) copy-start(bf16[16,32,188]{2,1,0:T(8,128)(2,1)} %param.9) | copy-start | bytes 577540
  81.4 44.5 %collective-permute-start.1 = (bf16[32,2048]{1,0:T(8,128)(2,1)}, bf16[32,2048]{1,0:T(8,128)(2,1)S(1)}, u32[]{:S(2)}, u32[]{:S(2)}) collective-permute-start(bf16[32,2048]{1,0:T(8,128)(2,1)} %get-tuple-element.42), channel_id=1, source_target_pairs={{8,0},{16,8},{24,16},{9,1},{17,9},{25,17},{10,2},{18,10},{26,18},{... | collective-permute-start | bytes 393224 | tf_op jit(solution)/shard_map/ppermute | solution.py:37
  82.6 43.2 %collective-permute-start = (bf16[32,2048]{1,0:T(8,128)(2,1)}, bf16[32,2048]{1,0:T(8,128)(2,1)}, u32[]{:S(2)}, u32[]{:S(2)}) collective-permute-start(bf16[32,2048]{1,0:T(8,128)(2,1)} %get-tuple-element.43), channel_id=1, source_target_pairs={{0,8},{8,16},{16,24},{1,9},{9,17},{17,25},{2,10},{10,18},{18,26},{... | collective-permute-start | bytes 393224 | tf_op jit(solution)/shard_map/ppermute | solution.py:37
  87.2 38.7 %collective-permute-start.2 = (bf16[16,2048]{1,0:T(8,128)(2,1)}, bf16[16,2048]{1,0:T(8,128)(2,1)S(1)}, u32[]{:S(2)}, u32[]{:S(2)}) collective-permute-start(bf16[16,2048]{1,0:T(8,128)(2,1)} %bitcast.68), channel_id=1, source_target_pairs={{0,1},{1,2},{2,3},{3,4},{4,5},{5,6},{6,7},{8,9},{9,10},{10,11},{11... | collective-permute-start | bytes 196616 | tf_op jit(solution)/shard_map/ppermute | solution.py:37
  91.6 34.2 %collective-permute-start.3 = (bf16[16,2048]{1,0:T(8,128)(2,1)}, bf16[16,2048]{1,0:T(8,128)(2,1)}, u32[]{:S(2)}, u32[]{:S(2)}) collective-permute-start(bf16[16,2048]{1,0:T(8,128)(2,1)} %bitcast.67), channel_id=1, source_target_pairs={{1,0},{2,1},{3,2},{4,3},{5,4},{6,5},{7,6},{9,8},{10,9},{11,10},{12... | collective-permute-start | bytes 196616 | tf_op jit(solution)/shard_map/ppermute | solution.py:37
  94.5 0.7 copy-start.16
  119.3 9.8 %copy-start.14 = (f32[2048]{0:T(1024)S(1)}, f32[2048]{0:T(1024)}, u32[]{:S(2)}) copy-start(f32[2048]{0:T(1024)} %param.17) | copy-start | bytes 24580
  138.6 52.1 %copy-start.6 = (bf16[512,512]{1,0:T(8,128)(2,1)S(1)}, bf16[512,512]{1,0:T(8,128)(2,1)}, u32[]{:S(2)}) copy-start(bf16[512,512]{1,0:T(8,128)(2,1)} %copy-done.5) | copy-start | bytes 1572868
  138.6 52.1 %copy-start.9 = (bf16[512,512]{1,0:T(8,128)(2,1)S(1)}, bf16[512,512]{1,0:T(8,128)(2,1)}, u32[]{:S(2)}) copy-start(bf16[512,512]{1,0:T(8,128)(2,1)} %copy-done.7) | copy-start | bytes 1572868
  194.6 1.3 copy-start.3
  195.9 52.4 %all-to-all-start.4 = ((bf16[8,512,256]{2,1,0:T(8,128)(2,1)}), bf16[8,512,256]{2,1,0:T(8,128)(2,1)}, u32[]{:S(2)}, u32[]{:S(2)}) async-start(bf16[8,512,256]{2,1,0:T(8,128)(2,1)} %bitcast.75), calls=%async_computation.4 | async-start | bytes 4194304 | tf_op jit(solution)/shard_map/all_to_all | solution.py:256
  200.6 19.0 %collective-permute-start.6 = (bf16[16,2048]{1,0:T(8,128)(2,1)S(1)}, bf16[16,2048]{1,0:T(8,128)(2,1)S(1)}, u32[]{:S(2)}, u32[]{:S(2)}) collective-permute-start(bf16[16,2048]{1,0:T(8,128)(2,1)S(1)} %bitcast.87), channel_id=1, source_target_pairs={{0,1},{1,2},{2,3},{3,4},{4,5},{5,6},{6,7},{8,9},{9,10},{10,11},{11... | collective-permute-start | bytes 196616 | tf_op jit(solution)/shard_map/ppermute | solution.py:37
  204.4 15.2 %collective-permute-start.7 = (bf16[16,2048]{1,0:T(8,128)(2,1)S(1)}, bf16[16,2048]{1,0:T(8,128)(2,1)S(1)}, u32[]{:S(2)}, u32[]{:S(2)}) collective-permute-start(bf16[16,2048]{1,0:T(8,128)(2,1)S(1)} %bitcast.86), channel_id=1, source_target_pairs={{1,0},{2,1},{3,2},{4,3},{5,4},{6,5},{7,6},{9,8},{10,9},{11,10},{12... | collective-permute-start | bytes 196616 | tf_op jit(solution)/shard_map/ppermute | solution.py:37
  205.7 14.5 %collective-permute-start.5 = (bf16[32,2048]{1,0:T(8,128)(2,1)S(1)}, bf16[32,2048]{1,0:T(8,128)(2,1)S(1)}, u32[]{:S(2)}, u32[]{:S(2)}) collective-permute-start(bf16[32,2048]{1,0:T(8,128)(2,1)S(1)} %get-tuple-element.38), channel_id=1, source_target_pairs={{8,0},{16,8},{24,16},{9,1},{17,9},{25,17},{10,2},{18,10},{26,18},{... | collective-permute-start | bytes 393224 | tf_op jit(solution)/shard_map/ppermute | solution.py:37
  207.0 13.2 %collective-permute-start.4 = (bf16[32,2048]{1,0:T(8,128)(2,1)S(1)}, bf16[32,2048]{1,0:T(8,128)(2,1)S(1)}, u32[]{:S(2)}, u32[]{:S(2)}) collective-permute-start(bf16[32,2048]{1,0:T(8,128)(2,1)S(1)} %get-tuple-element.39), channel_id=1, source_target_pairs={{0,8},{8,16},{16,24},{1,9},{9,17},{17,25},{2,10},{10,18},{18,26},{... | collective-permute-start | bytes 393224 | tf_op jit(solution)/shard_map/ppermute | solution.py:37
  219.6 0.6 copy-start.12
  220.2 0.7 copy-start.10
  248.3 0.9 copy-start.11
  249.2 0.8 copy-start.13

commit v4 on v3

--- a/solution.py
+++ b/solution.py
@@ -112,7 +112,8 @@
         preferred_element_type=jnp.float32,
     )
     back = jnp.dot(solved.astype(jnp.bfloat16), library, preferred_element_type=jnp.float32)
-    out_ref[...] = (right - back) / MU
+    primal = (right - back) / MU
+    out_ref[...] = primal - rest[0][...] if len(rest) > 1 else primal
 
 
 def primal_step(observed, library, inverse, tile, dual):
@@ -144,16 +145,16 @@
     )(*arrays)
 
 
-def update_kernel(has_dual, keep_dual, *refs):
-    primal_ref, averaged_ref, tile_ref, top_ref, bottom_ref, left_ref, right_ref, threshold_ref = (
+def update_kernel(keep_dual, *refs):
+    base_ref, averaged_ref, tile_ref, top_ref, bottom_ref, left_ref, right_ref, threshold_ref = (
         refs[:8]
     )
     refs = refs[8:]
-    dual_ref = refs[0] if has_dual else None
-    fresh_ref = refs[1 if has_dual else 0]
+    fresh_ref = refs[0]
     new_ref, strip_ref = refs[-2:] if keep_dual else (None, None)
     rows, columns, atoms = tile_ref.shape
     threshold = threshold_ref[...]
+    share = 1.0 / (1.0 + GAMMA + ETA)
     left = left_ref[...].astype(jnp.float32)
     right = right_ref[...].astype(jnp.float32)
     place = lax.broadcasted_iota(jnp.int32, (columns, atoms), 0)
@@ -164,12 +165,12 @@
         below = (tile_ref[row + 1] if row + 1 < rows else bottom_ref[...]).astype(jnp.float32)
         west = jnp.where(place == 0, left[row : row + 1], pltpu.roll(here, 1, 0))
         east = jnp.where(place == columns - 1, right[row : row + 1], pltpu.roll(here, columns - 1, 0))
-        spatial = 0.25 * (above + below + west + east)
+        spatial = above + below + west + east
         pixels = pl.ds(row * columns, columns)
-        primal = primal_ref[pixels]
-        base = primal - dual_ref[pixels] if has_dual else primal
-        averaged = jnp.sqrt(jnp.sqrt(averaged_ref[0, pixels].astype(jnp.float32)))
-        blend = (base + GAMMA * averaged + ETA * spatial) / (1.0 + GAMMA + ETA)
+        base = base_ref[pixels]
+        powers = jnp.maximum(averaged_ref[0, pixels].astype(jnp.float32), 1e-36)
+        averaged = lax.rsqrt(lax.rsqrt(powers))
+        blend = share * base + (share * GAMMA) * averaged + (share * ETA * 0.25) * spatial
         fresh = jnp.maximum(blend - threshold, 0.0)
         rounded = fresh.astype(jnp.bfloat16)
         fresh_ref[pixels] = rounded
@@ -179,7 +180,7 @@
         above, here = here, below
 
 
-def update(primal, averaged, tile, halo, threshold, dual, keep_dual):
+def update(base, averaged, tile, halo, threshold, keep_dual):
     rows, columns, atoms = tile.shape
     pixels = rows * columns
     width = averaged.shape[2]
@@ -188,16 +189,13 @@
     specs = [flat, strip, pl.BlockSpec((rows, columns, width), lambda i: (0, 0, i))]
     specs += [pl.BlockSpec((part.shape[0], width), lambda i: (0, i)) for part in halo]
     specs += [pl.BlockSpec((1, width), lambda i: (0, i))]
-    arrays = [primal, averaged, tile, *halo, threshold.reshape(1, -1)]
-    if dual is not None:
-        specs.append(flat)
-        arrays.append(dual)
+    arrays = [base, averaged, tile, *halo, threshold.reshape(1, -1)]
     shapes = [jax.ShapeDtypeStruct((pixels, atoms), jnp.bfloat16)]
     if keep_dual:
         shapes.append(jax.ShapeDtypeStruct((pixels, atoms), jnp.float32))
         shapes.append(jax.ShapeDtypeStruct(averaged.shape, jnp.bfloat16))
     return pl.pallas_call(
-        functools.partial(update_kernel, dual is not None, keep_dual),
+        functools.partial(update_kernel, keep_dual),
         out_shape=shapes,
         grid=(atoms // width,),
         in_specs=specs,
@@ -228,9 +226,15 @@
     part = jnp.sum(
         jnp.where(hit[None], coef.reshape(blocks, group, slots)[:, :, :, None], 0.0), axis=2
     ).reshape(1, blocks, group * blocks)
-    parts = jnp.broadcast_to(part, (group,) + part.shape[1:])
-    weights = lax.all_to_all(parts, "col", split_axis=0, concat_axis=0, tiled=True)
-    weights = weights.reshape(group * blocks, group * blocks)
+    me = lax.axis_index("col")
+    got = [part]
+    for ahead in range(1, group):
+        got.append(lax.ppermute(part, "col", [(i, (i + ahead) % group) for i in range(group)]))
+    steps = jnp.arange(group, dtype=jnp.int32)
+    mine = steps[:, None] == lax.rem(me - steps + group, group)[None, :]
+    weights = jnp.sum(
+        jnp.where(mine[:, :, None, None], jnp.concatenate(got, axis=0)[None], 0.0), axis=1
+    ).reshape(group * blocks, group * blocks)
     high, low = spread(weights)
 
     bands = library.shape[0]
@@ -259,10 +263,10 @@
         top, bottom = beside(current, "row", 0)
         left, right = beside(current, "col", 1)
         flat = current.reshape(pixels, atoms)
-        primal = primal_step(seen, library, inverse, flat, dual)
+        base = primal_step(seen, library, inverse, flat, dual)
         keep = step + 1 < ITERS
         out = update(
-            primal, averaged, current, (top, bottom, left, right), threshold, dual, keep
+            base, averaged, current, (top, bottom, left, right), threshold, keep
         )
         if keep:
             dual, strips = out[1:]

time: 264 us -> 261 us (0.989)
  starting transfers between devices: 39.5 us -> 52.8 us
  waiting for transfers between devices: 48 us -> 38.4 us
  other arithmetic: 56.4 us -> 53.1 us
  Pallas kernels: 41.9 us -> 39.2 us
    ppermute x0 -> x7, starting transfers between devices: none -> 14 us  [local(): lax.ppermute(part, 'col', [(i, (i + ahead) % group) for i in range(group)])]
    all_to_all x1, waiting for transfers between devices: 13.5 us -> 0.01 us  [local(): lax.all_to_all(strips, 'col', split_axis=0, concat_axis=0, tiled=True)]
    all_to_all x1 -> x0, starting transfers between devices: 7.25 us -> none  [local(): lax.all_to_all(parts, 'col', split_axis=0, concat_axis=0, tiled=True)]
    ppermute x0 -> x7, waiting for transfers between devices: none -> 6.78 us  [local(): lax.ppermute(part, 'col', [(i, (i + ahead) % group) for i in range(group)])]
    all_to_all x1, starting transfers between devices: 3.75 us -> 7.4 us  [local(): lax.all_to_all(strips, 'col', split_axis=0, concat_axis=0, tiled=True)]
    all_to_all x2, starting transfers between devices: 8.84 us -> 11.7 us  [local(): lax.all_to_all(sums.reshape(strips.shape), 'col', split_axis=0, concat_ax...]
    unnamed x41 -> x56, local copies, waits for them, and re-layouts: 12.6 us -> 12.1 us
  transfers between devices with their start and end apart: 12 -> 18, of which waited for: 5 -> 5; matrix products, arithmetic and copies ran while one was open for 24% -> 23% of each run, Pallas kernels for 6% -> 6%
where the time goes in v4:
time: 261 us; the launch traced here: 260 us
  other arithmetic  53.1 us (20%)
  starting transfers between devices  52.8 us (20%)
  blocking collectives  52.8 us (20%)
  Pallas kernels  39.2 us (15%)
  waiting for transfers between devices  38.4 us (15%)
  local copies, waits for them, and re-layouts  15.5 us (6%)
  matrix products  5.97 us (2%)
    all_to_all x1, blocking collectives, local(): lax.all_to_all(strips, 'col', split_axis=0, concat_axis=0, tiled=True)  52.8 us
    all_to_all x2, waiting for transfers between devices, local(): lax.all_to_all(sums.reshape(strips.shape), 'col', split_axis=0, concat_ax...  30 us
    another operation x7, other arithmetic, local(): chol = jnp.linalg.cholesky(gram)  28.4 us
    another operation x6, other arithmetic, local(): jax.scipy.linalg.solve_triangular(chol, jnp.eye(bands, dtype=jnp.float32)...  21.3 us
    pallas_call x2, Pallas kernels, update(): pl.pallas_call(functools.partial(update_kernel, keep_dual), out_shape=sha...  16.5 us
    ppermute x4, starting transfers between devices, beside(): lax.ppermute(last, axis, forward)  14.4 us
    pallas_call x2, Pallas kernels, primal_step(): pl.pallas_call(primal_kernel, out_shape=jax.ShapeDtypeStruct((pixels, ato...  14.4 us
    ppermute x7, starting transfers between devices, local(): lax.ppermute(part, 'col', [(i, (i + ahead) % group) for i in range(group)])  14 us
  transfers between devices with their start and end apart: 18, of which 5 were waited for; matrix products, arithmetic and copies ran while one was open for 23% of the time, Pallas kernels for 6%

profile of v4, /device:TPU:0, one launch (start us, length us, event | category | flops | bytes accessed | tf_op | source)
XLA Modules:
  0.0 260.1 jit_solution(17831525626920344067)
XLA Ops:
  0.6 2.3 copy.46
  2.9 1.7 copy.52
  4.7 7.4 %all-to-all-start = ((bf16[8,512,256]{2,1,0:T(8,128)(2,1)}), bf16[8,512,256]{2,1,0:T(8,128)(2,1)S(1)}, u32[]{:S(2)}, u32[]{:S(2)}) async-start(bf16[8,512,256]{2,1,0:T(8,128)(2,1)} %bitcast.82), calls=%async_computation | async-start | bytes 4194304 | tf_op jit(solution)/shard_map/all_to_all | solution.py:250
  12.9 4.7 %collective-permute-start.6 = (f32[1,4,32]{2,1,0:T(4,128)S(1)}, f32[1,4,32]{2,1,0:T(4,128)S(1)}, u32[]{:S(2)}, u32[]{:S(2)}) collective-permute-start(f32[1,4,32]{2,1,0:T(4,128)S(1)} %reshape.170), channel_id=1, source_target_pairs={{0,7},{1,0},{2,1},{3,2},{4,3},{5,4},{6,5},{7,6},{8,15},{9,8},{10,9... | collective-permute-start | bytes 1544 | tf_op jit(solution)/shard_map/ppermute | solution.py:232
  18.2 2.9 %collective-permute-start.3 = (f32[1,4,32]{2,1,0:T(4,128)S(1)}, f32[1,4,32]{2,1,0:T(4,128)S(1)}, u32[]{:S(2)}, u32[]{:S(2)}) collective-permute-start(f32[1,4,32]{2,1,0:T(4,128)S(1)} %reshape.170), channel_id=1, source_target_pairs={{0,4},{1,5},{2,6},{3,7},{4,0},{5,1},{6,2},{7,3},{8,12},{9,13},{10,... | collective-permute-start | bytes 1544 | tf_op jit(solution)/shard_map/ppermute | solution.py:232
  21.1 1.5 collective-permute-start
  23.1 11.7 %cholesky.51 = f32[128,128]{1,0:T(8,128)S(1)} custom-call(f32[128,128]{1,0:T(8,128)S(1)} %cholesky.124), custom_call_target="Cholesky" | custom-call | tf_op jit(solution)/shard_map/jit(cholesky)/cholesky | solution.py:244
  34.9 9.8 %custom-call.15 = f32[1,128,128]{1,2,0:T(8,128)S(1)} custom-call(f32[1,128,128]{2,1,0:T(8,128)S(1)} %get-tuple-element.45), custom_call_target="InvertDiagBlocksLowerTriangular" | custom-call | tf_op jit(solution)/shard_map/jit(cholesky)/cholesky | solution.py:244
  45.1 5.5 %cholesky.110 = f32[60,60]{1,0:T(8,128)S(1)} custom-call(f32[60,60]{1,0:T(8,128)S(1)} %convolution_subtract_fusion.1), custom_call_target="Cholesky" | custom-call | tf_op jit(solution)/shard_map/jit(cholesky)/cholesky | solution.py:244
  53.9 5.5 %collective-permute-done.1 = f32[1,4,32]{2,1,0:T(4,128)S(1)} collective-permute-done((f32[1,4,32]{2,1,0:T(4,128)S(1)}, f32[1,4,32]{2,1,0:T(4,128)S(1)}, u32[]{:S(2)}, u32[]{:S(2)}) %collective-permute-start.1) | collective-permute-done | bytes 544 | tf_op jit(solution)/shard_map/ppermute | solution.py:232
  59.4 4.3 %collective-permute-start.2 = (f32[1,4,32]{2,1,0:T(4,128)S(1)}, f32[1,4,32]{2,1,0:T(4,128)S(1)}, u32[]{:S(2)}, u32[]{:S(2)}) collective-permute-start(f32[1,4,32]{2,1,0:T(4,128)S(1)} %reshape.170), channel_id=1, source_target_pairs={{0,3},{1,4},{2,5},{3,6},{4,7},{5,0},{6,1},{7,2},{8,11},{9,12},{10,... | collective-permute-start | bytes 1544 | tf_op jit(solution)/shard_map/ppermute | solution.py:232
  68.0 3.8 %mix.2 = bf16[32,128,256]{2,1,0:T(8,128)(2,1)S(1)} custom-call(bf16[512,512]{1,0:T(8,128)(2,1)S(1)} %get-tuple-element.10.high_ref, bf16[512,512]{1,0:T(8,128)(2,1)S(1)} %copy-done.8, bf16[32,128,256]{2,1,0:T(8,128)(2,1)S(1)} %bitcast.73), custom_call_target="tpu_custom_call" | custom-call | tf_op jit(solution)/shard_map/mix/pallas_call | solution.py:83
  71.8 1.3 copy-done.2
  73.1 7.3 %all-to-all-start.1 = ((bf16[8,512,256]{2,1,0:T(8,128)(2,1)}), bf16[8,512,256]{2,1,0:T(8,128)(2,1)}, u32[]{:S(2)}, u32[]{:S(2)}) async-start(bf16[8,512,256]{2,1,0:T(8,128)(2,1)} %bitcast.74), calls=%async_computation.1 | async-start | bytes 4194304 | tf_op jit(solution)/shard_map/all_to_all | solution.py:260
  82.5 3.7 %collective-permute-start.7 = (bf16[32,2048]{1,0:T(8,128)(2,1)}, bf16[32,2048]{1,0:T(8,128)(2,1)}, u32[]{:S(2)}, u32[]{:S(2)}) collective-permute-start(bf16[32,2048]{1,0:T(8,128)(2,1)} %get-tuple-element.43), channel_id=1, source_target_pairs={{0,8},{8,16},{16,24},{1,9},{9,17},{17,25},{2,10},{10,18},{18,26},{... | collective-permute-start | bytes 393224 | tf_op jit(solution)/shard_map/ppermute | solution.py:37
  87.1 3.9 %collective-permute-start.9 = (bf16[16,2048]{1,0:T(8,128)(2,1)}, bf16[16,2048]{1,0:T(8,128)(2,1)S(1)}, u32[]{:S(2)}, u32[]{:S(2)}) collective-permute-start(bf16[16,2048]{1,0:T(8,128)(2,1)} %bitcast.68), channel_id=1, source_target_pairs={{0,1},{1,2},{2,3},{3,4},{4,5},{5,6},{6,7},{8,9},{9,10},{10,11},{11... | collective-permute-start | bytes 196616 | tf_op jit(solution)/shard_map/ppermute | solution.py:37
  91.6 1.5 collective-permute-start.10
  95.9 20.5 %custom-call.16 = f32[2,128,128]{1,2,0:T(8,128)S(1)} custom-call(f32[2,128,128]{2,1,0:T(8,128)} %pad_maximum_fusion), custom_call_target="InvertDiagBlocksLowerTriangular" | custom-call | tf_op jit(solution)/shard_map/jit(_solve_triangular)/triangular_solve | solution.py:253
  119.3 6.4 %primal.2.refs_0_ = f32[512,2048]{1,0:T(8,128)} custom-call(bf16[512,188]{1,0:T(8,128)(2,1)S(1)} %bitcast.77, bf16[188,2048]{1,0:T(8,128)(2,1)S(1)} %copy-done.1, f32[188,188]{1,0:T(8,128)S(1)} %fusion.inverse_ref, bf16[512,2048]{1,0:T(8,128)(2,1)S(1)} %bitcast.70), custom_call_target="tpu_custom_call" | custom-call | flops 1577058304 | bytes 12582912 | tf_op jit(solution)/shard_map/primal/pallas_call | solution.py:134
  125.8 2.6 all-to-all-done.1.refs_1_
  128.4 8.8 %update.2 = (bf16[512,2048]{1,0:T(8,128)(2,1)S(1)}, f32[512,2048]{1,0:T(8,128)}, bf16[8,512,256]{2,1,0:T(8,128)(2,1)S(1)}) custom-call(f32[512,2048]{1,0:T(8,128)} %primal.2.refs_0_, bf16[8,512,256]{2,1,0:T(8,128)(2,1)} %all-to-all-done.1.refs_1_, bf16[16,32,2048]{2,1,0:T(8,128)(2,1)} %refs_2_.1, bf16[32,2048]{1,0:T(8,128)(2,1)} %collective-permute-done.7.refs_3_, ...), custom_call_target="tpu_custom_call" | custom-call | tf_op jit(solution)/shard_map/update/pallas_call | solution.py:197
  137.2 52.8 %all_to_all.20 = bf16[8,512,256]{2,1,0:T(8,128)(2,1)S(1)} all-to-all(bf16[8,512,256]{2,1,0:T(8,128)(2,1)S(1)} %get-tuple-element.15), channel_id=1, replica_groups=mesh['row'=4,'col'=8] {'col'}, dimensions={0} | all-to-all | bytes 4194304 | tf_op jit(solution)/shard_map/all_to_all | solution.py:250
  190.0 3.8 %mix.3 = bf16[32,128,256]{2,1,0:T(8,128)(2,1)S(1)} custom-call(bf16[512,512]{1,0:T(8,128)(2,1)S(1)} %copy-done.6, bf16[512,512]{1,0:T(8,128)(2,1)S(1)} %copy-done.9, bf16[32,128,256]{2,1,0:T(8,128)(2,1)S(1)} %bitcast.76), custom_call_target="tpu_custom_call" | custom-call | tf_op jit(solution)/shard_map/mix/pallas_call | solution.py:83
  193.8 1.3 copy-done.3
  195.1 4.4 %all-to-all-start.3 = ((bf16[8,512,256]{2,1,0:T(8,128)(2,1)}), bf16[8,512,256]{2,1,0:T(8,128)(2,1)}, u32[]{:S(2)}, u32[]{:S(2)}) async-start(bf16[8,512,256]{2,1,0:T(8,128)(2,1)} %bitcast.75), calls=%async_computation.3 | async-start | bytes 4194304 | tf_op jit(solution)/shard_map/all_to_all | solution.py:260
  199.8 3.8 %collective-permute-start.13 = (bf16[16,2048]{1,0:T(8,128)(2,1)S(1)}, bf16[16,2048]{1,0:T(8,128)(2,1)S(1)}, u32[]{:S(2)}, u32[]{:S(2)}) collective-permute-start(bf16[16,2048]{1,0:T(8,128)(2,1)S(1)} %bitcast.87), channel_id=1, source_target_pairs={{0,1},{1,2},{2,3},{3,4},{4,5},{5,6},{6,7},{8,9},{9,10},{10,11},{11... | collective-permute-start | bytes 196616 | tf_op jit(solution)/shard_map/ppermute | solution.py:37
  206.2 3.0 %collective-permute-start.11 = (bf16[32,2048]{1,0:T(8,128)(2,1)S(1)}, bf16[32,2048]{1,0:T(8,128)(2,1)S(1)}, u32[]{:S(2)}, u32[]{:S(2)}) collective-permute-start(bf16[32,2048]{1,0:T(8,128)(2,1)S(1)} %get-tuple-element.39), channel_id=1, source_target_pairs={{0,8},{8,16},{16,24},{1,9},{9,17},{17,25},{2,10},{10,18},{18,26},{... | collective-permute-start | bytes 393224 | tf_op jit(solution)/shard_map/ppermute | solution.py:37
  209.3 8.0 %primal.3.refs_0_ = f32[512,2048]{1,0:T(8,128)} custom-call(bf16[512,188]{1,0:T(8,128)(2,1)S(1)} %bitcast.78, bf16[188,2048]{1,0:T(8,128)(2,1)S(1)} %copy-done.1, f32[188,188]{1,0:T(8,128)S(1)} %fusion.inverse_ref, bf16[512,2048]{1,0:T(8,128)(2,1)S(1)} %get-tuple-element.13.tile_ref, f32[512,2048]{1,0:T(8,128)} %get-tuple-element.14.rest_0_), custom_call_target="tpu_custom_call" | custom-call | flops 1577058304 | bytes 12582912 | tf_op jit(solution)/shard_map/primal/pallas_call | solution.py:134
  217.3 1.5 collective-permute-done.13.refs_5_
  220.1 27.5 %all-to-all-done.3.refs_1_ = bf16[8,512,256]{2,1,0:T(8,128)(2,1)} async-done(((bf16[8,512,256]{2,1,0:T(8,128)(2,1)}), bf16[8,512,256]{2,1,0:T(8,128)(2,1)}, u32[]{:S(2)}, u32[]{:S(2)}) %all-to-all-start.3) | async-done | bytes 2097184 | tf_op jit(solution)/shard_map/all_to_all | solution.py:260
  249.3 7.7 %update.3 = bf16[512,2048]{1,0:T(8,128)(2,1)} custom-call(f32[512,2048]{1,0:T(8,128)} %primal.3.refs_0_, bf16[8,512,256]{2,1,0:T(8,128)(2,1)} %all-to-all-done.3.refs_1_, bf16[16,32,2048]{2,1,0:T(8,128)(2,1)S(1)} %bitcast.72, bf16[32,2048]{1,0:T(8,128)(2,1)S(1)} %copy-done.11, bf16[32,2048]{1,0:T(8,128)(2,1)S(1)} %collective-permute-done.12.refs_4_, ...), custom_call_target="tpu_custom_call" | custom-call | tf_op jit(solution)/shard_map/update/pallas_call | solution.py:197
  256.9 2.3 fusion.25
  (118 shorter events, 24.6 us)
Async XLA Ops:
  4.6 7.4 %copy-start.17 = (f32[4,1,8]{2,1,0:T(1,128)S(1)}, f32[4,1,8]{2,1,0:T(1,128)}, u32[]{:S(2)}) copy-start(f32[4,1,8]{2,1,0:T(1,128)} %param.15) | copy-start | bytes 388
  4.6 7.4 %copy-start.20 = (s32[4,1]{0,1:T(1,128)S(1)}, s32[4,1]{0,1:T(1,128)}, u32[]{:S(2)}) copy-start(s32[4,1]{0,1:T(1,128)} %param.14) | copy-start | bytes 52
  4.6 7.6 %copy-start.18 = (s32[4,1,8]{2,1,0:T(1,128)S(1)}, s32[4,1,8]{2,1,0:T(1,128)}, u32[]{:S(2)}) copy-start(s32[4,1,8]{2,1,0:T(1,128)} %param.13) | copy-start | bytes 388
  4.6 7.6 %copy-start.19 = (s32[4,1,8]{2,1,0:T(1,128)S(1)}, s32[4,1,8]{2,1,0:T(1,128)}, u32[]{:S(2)}) copy-start(s32[4,1,8]{2,1,0:T(1,128)} %param.12) | copy-start | bytes 388
  4.7 8.0 %copy-start.21 = (s32[1,8,2]{1,2,0:T(2,128)S(1)}, s32[1,8,2]{1,2,0:T(2,128)}, u32[]{:S(2)}) copy-start(s32[1,8,2]{1,2,0:T(2,128)} %param.16) | copy-start | bytes 196
  4.7 17.9 %copy-start.1 = (bf16[188,2048]{1,0:T(8,128)(2,1)S(1)}, bf16[188,2048]{1,0:T(8,128)(2,1)}, u32[]{:S(2)}) copy-start(bf16[188,2048]{1,0:T(8,128)(2,1)} %library_ref.3) | copy-start | bytes 2310148
  4.7 62.1 %all-to-all-start = ((bf16[8,512,256]{2,1,0:T(8,128)(2,1)}), bf16[8,512,256]{2,1,0:T(8,128)(2,1)S(1)}, u32[]{:S(2)}, u32[]{:S(2)}) async-start(bf16[8,512,256]{2,1,0:T(8,128)(2,1)} %bitcast.82), calls=%async_computation | async-start | bytes 4194304 | tf_op jit(solution)/shard_map/all_to_all | solution.py:250
  12.9 52.2 %collective-permute-start.6 = (f32[1,4,32]{2,1,0:T(4,128)S(1)}, f32[1,4,32]{2,1,0:T(4,128)S(1)}, u32[]{:S(2)}, u32[]{:S(2)}) collective-permute-start(f32[1,4,32]{2,1,0:T(4,128)S(1)} %reshape.170), channel_id=1, source_target_pairs={{0,7},{1,0},{2,1},{3,2},{4,3},{5,4},{6,5},{7,6},{8,15},{9,8},{10,9... | collective-permute-start | bytes 1544 | tf_op jit(solution)/shard_map/ppermute | solution.py:232
  17.6 47.5 %collective-permute-start.5 = (f32[1,4,32]{2,1,0:T(4,128)S(1)}, f32[1,4,32]{2,1,0:T(4,128)S(1)}, u32[]{:S(2)}, u32[]{:S(2)}) collective-permute-start(f32[1,4,32]{2,1,0:T(4,128)S(1)} %reshape.170), channel_id=1, source_target_pairs={{0,6},{1,7},{2,0},{3,1},{4,2},{5,3},{6,4},{7,5},{8,14},{9,15},{10,... | collective-permute-start | bytes 1544 | tf_op jit(solution)/shard_map/ppermute | solution.py:232
  18.2 46.9 %collective-permute-start.4 = (f32[1,4,32]{2,1,0:T(4,128)S(1)}, f32[1,4,32]{2,1,0:T(4,128)S(1)}, u32[]{:S(2)}, u32[]{:S(2)}) collective-permute-start(f32[1,4,32]{2,1,0:T(4,128)S(1)} %reshape.170), channel_id=1, source_target_pairs={{0,5},{1,6},{2,7},{3,0},{4,1},{5,2},{6,3},{7,4},{8,13},{9,14},{10,... | collective-permute-start | bytes 1544 | tf_op jit(solution)/shard_map/ppermute | solution.py:232
  18.2 46.9 %collective-permute-start.3 = (f32[1,4,32]{2,1,0:T(4,128)S(1)}, f32[1,4,32]{2,1,0:T(4,128)S(1)}, u32[]{:S(2)}, u32[]{:S(2)}) collective-permute-start(f32[1,4,32]{2,1,0:T(4,128)S(1)} %reshape.170), channel_id=1, source_target_pairs={{0,4},{1,5},{2,6},{3,7},{4,0},{5,1},{6,2},{7,3},{8,12},{9,13},{10,... | collective-permute-start | bytes 1544 | tf_op jit(solution)/shard_map/ppermute | solution.py:232
  21.1 32.8 %collective-permute-start = (f32[1,4,32]{2,1,0:T(4,128)S(1)}, f32[1,4,32]{2,1,0:T(4,128)S(1)}, u32[]{:S(2)}, u32[]{:S(2)}) collective-permute-start(f32[1,4,32]{2,1,0:T(4,128)S(1)} %reshape.170), channel_id=1, source_target_pairs={{0,1},{1,2},{2,3},{3,4},{4,5},{5,6},{6,7},{7,0},{8,9},{9,10},{10,1... | collective-permute-start | bytes 1544 | tf_op jit(solution)/shard_map/ppermute | solution.py:232
  53.9 5.5 %collective-permute-start.1 = (f32[1,4,32]{2,1,0:T(4,128)S(1)}, f32[1,4,32]{2,1,0:T(4,128)S(1)}, u32[]{:S(2)}, u32[]{:S(2)}) collective-permute-start(f32[1,4,32]{2,1,0:T(4,128)S(1)} %reshape.170), channel_id=1, source_target_pairs={{0,2},{1,3},{2,4},{3,5},{4,6},{5,7},{6,0},{7,1},{8,10},{9,11},{10,... | collective-permute-start | bytes 1544 | tf_op jit(solution)/shard_map/ppermute | solution.py:232
  59.4 5.6 %collective-permute-start.2 = (f32[1,4,32]{2,1,0:T(4,128)S(1)}, f32[1,4,32]{2,1,0:T(4,128)S(1)}, u32[]{:S(2)}, u32[]{:S(2)}) collective-permute-start(f32[1,4,32]{2,1,0:T(4,128)S(1)} %reshape.170), channel_id=1, source_target_pairs={{0,3},{1,4},{2,5},{3,6},{4,7},{5,0},{6,1},{7,2},{8,11},{9,12},{10,... | collective-permute-start | bytes 1544 | tf_op jit(solution)/shard_map/ppermute | solution.py:232
  66.7 5.1 %copy-start.5 = (bf16[512,512]{1,0:T(8,128)(2,1)}, bf16[512,512]{1,0:T(8,128)(2,1)S(1)}, u32[]{:S(2)}) copy-start(bf16[512,512]{1,0:T(8,128)(2,1)S(1)} %get-tuple-element.10.high_ref) | copy-start | bytes 1572868
  71.8 1.3 copy-start.2
  73.1 7.3 %copy-start = (bf16[16,32,2048]{2,1,0:T(8,128)(2,1)S(1)}, bf16[16,32,2048]{2,1,0:T(8,128)(2,1)}, u32[]{:S(2)}) copy-start(bf16[16,32,2048]{2,1,0:T(8,128)(2,1)} %refs_2_.1) | copy-start | bytes 6291460
  73.1 21.3 %copy-start.15 = (f32[188,188]{1,0:T(8,128)S(1)}, f32[188,188]{1,0:T(8,128)}, u32[]{:S(2)}) copy-start(f32[188,188]{1,0:T(8,128)} %select_select_fusion) | copy-start | bytes 424132
  73.1 55.2 %all-to-all-start.1 = ((bf16[8,512,256]{2,1,0:T(8,128)(2,1)}), bf16[8,512,256]{2,1,0:T(8,128)(2,1)}, u32[]{:S(2)}, u32[]{:S(2)}) async-start(bf16[8,512,256]{2,1,0:T(8,128)(2,1)} %bitcast.74), calls=%async_computation.1 | async-start | bytes 4194304 | tf_op jit(solution)/shard_map/all_to_all | solution.py:260
  80.5 38.8 %copy-start.4 = (bf16[16,32,188]{2,1,0:T(8,128)(2,1)S(1)}, bf16[16,32,188]{2,1,0:T(8,128)(2,1)}, u32[]{:S(2)}) copy-start(bf16[16,32,188]{2,1,0:T(8,128)(2,1)} %param.9) | copy-start | bytes 577540
  81.2 44.6 %collective-permute-start.8 = (bf16[32,2048]{1,0:T(8,128)(2,1)}, bf16[32,2048]{1,0:T(8,128)(2,1)S(1)}, u32[]{:S(2)}, u32[]{:S(2)}) collective-permute-start(bf16[32,2048]{1,0:T(8,128)(2,1)} %get-tuple-element.42), channel_id=1, source_target_pairs={{8,0},{16,8},{24,16},{9,1},{17,9},{25,17},{10,2},{18,10},{26,18},{... | collective-permute-start | bytes 393224 | tf_op jit(solution)/shard_map/ppermute | solution.py:37
  82.5 43.3 %collective-permute-start.7 = (bf16[32,2048]{1,0:T(8,128)(2,1)}, bf16[32,2048]{1,0:T(8,128)(2,1)}, u32[]{:S(2)}, u32[]{:S(2)}) collective-permute-start(bf16[32,2048]{1,0:T(8,128)(2,1)} %get-tuple-element.43), channel_id=1, source_target_pairs={{0,8},{8,16},{16,24},{1,9},{9,17},{17,25},{2,10},{10,18},{18,26},{... | collective-permute-start | bytes 393224 | tf_op jit(solution)/shard_map/ppermute | solution.py:37
  87.1 38.7 %collective-permute-start.9 = (bf16[16,2048]{1,0:T(8,128)(2,1)}, bf16[16,2048]{1,0:T(8,128)(2,1)S(1)}, u32[]{:S(2)}, u32[]{:S(2)}) collective-permute-start(bf16[16,2048]{1,0:T(8,128)(2,1)} %bitcast.68), channel_id=1, source_target_pairs={{0,1},{1,2},{2,3},{3,4},{4,5},{5,6},{6,7},{8,9},{9,10},{10,11},{11... | collective-permute-start | bytes 196616 | tf_op jit(solution)/shard_map/ppermute | solution.py:37
  91.6 34.1 %collective-permute-start.10 = (bf16[16,2048]{1,0:T(8,128)(2,1)}, bf16[16,2048]{1,0:T(8,128)(2,1)}, u32[]{:S(2)}, u32[]{:S(2)}) collective-permute-start(bf16[16,2048]{1,0:T(8,128)(2,1)} %bitcast.67), channel_id=1, source_target_pairs={{1,0},{2,1},{3,2},{4,3},{5,4},{6,5},{7,6},{9,8},{10,9},{11,10},{12... | collective-permute-start | bytes 196616 | tf_op jit(solution)/shard_map/ppermute | solution.py:37
  119.3 9.0 %copy-start.14 = (f32[2048]{0:T(1024)S(1)}, f32[2048]{0:T(1024)}, u32[]{:S(2)}) copy-start(f32[2048]{0:T(1024)} %param.17) | copy-start | bytes 24580
  137.2 52.8 %copy-start.6 = (bf16[512,512]{1,0:T(8,128)(2,1)S(1)}, bf16[512,512]{1,0:T(8,128)(2,1)}, u32[]{:S(2)}) copy-start(bf16[512,512]{1,0:T(8,128)(2,1)} %copy-done.5) | copy-start | bytes 1572868
  137.2 52.8 %copy-start.9 = (bf16[512,512]{1,0:T(8,128)(2,1)S(1)}, bf16[512,512]{1,0:T(8,128)(2,1)}, u32[]{:S(2)}) copy-start(bf16[512,512]{1,0:T(8,128)(2,1)} %copy-done.7) | copy-start | bytes 1572868
  195.1 52.4 %all-to-all-start.3 = ((bf16[8,512,256]{2,1,0:T(8,128)(2,1)}), bf16[8,512,256]{2,1,0:T(8,128)(2,1)}, u32[]{:S(2)}, u32[]{:S(2)}) async-start(bf16[8,512,256]{2,1,0:T(8,128)(2,1)} %bitcast.75), calls=%async_computation.3 | async-start | bytes 4194304 | tf_op jit(solution)/shard_map/all_to_all | solution.py:260
  199.8 19.0 %collective-permute-start.13 = (bf16[16,2048]{1,0:T(8,128)(2,1)S(1)}, bf16[16,2048]{1,0:T(8,128)(2,1)S(1)}, u32[]{:S(2)}, u32[]{:S(2)}) collective-permute-start(bf16[16,2048]{1,0:T(8,128)(2,1)S(1)} %bitcast.87), channel_id=1, source_target_pairs={{0,1},{1,2},{2,3},{3,4},{4,5},{5,6},{6,7},{8,9},{9,10},{10,11},{11... | collective-permute-start | bytes 196616 | tf_op jit(solution)/shard_map/ppermute | solution.py:37
  203.6 15.2 %collective-permute-start.14 = (bf16[16,2048]{1,0:T(8,128)(2,1)S(1)}, bf16[16,2048]{1,0:T(8,128)(2,1)S(1)}, u32[]{:S(2)}, u32[]{:S(2)}) collective-permute-start(bf16[16,2048]{1,0:T(8,128)(2,1)S(1)} %bitcast.86), channel_id=1, source_target_pairs={{1,0},{2,1},{3,2},{4,3},{5,4},{6,5},{7,6},{9,8},{10,9},{11,10},{12... | collective-permute-start | bytes 196616 | tf_op jit(solution)/shard_map/ppermute | solution.py:37
  204.9 14.5 %collective-permute-start.12 = (bf16[32,2048]{1,0:T(8,128)(2,1)S(1)}, bf16[32,2048]{1,0:T(8,128)(2,1)S(1)}, u32[]{:S(2)}, u32[]{:S(2)}) collective-permute-start(bf16[32,2048]{1,0:T(8,128)(2,1)S(1)} %get-tuple-element.38), channel_id=1, source_target_pairs={{8,0},{16,8},{24,16},{9,1},{17,9},{25,17},{10,2},{18,10},{26,18},{... | collective-permute-start | bytes 393224 | tf_op jit(solution)/shard_map/ppermute | solution.py:37
  206.2 13.2 %collective-permute-start.11 = (bf16[32,2048]{1,0:T(8,128)(2,1)S(1)}, bf16[32,2048]{1,0:T(8,128)(2,1)S(1)}, u32[]{:S(2)}, u32[]{:S(2)}) collective-permute-start(bf16[32,2048]{1,0:T(8,128)(2,1)S(1)} %get-tuple-element.39), channel_id=1, source_target_pairs={{0,8},{8,16},{16,24},{1,9},{9,17},{17,25},{2,10},{10,18},{18,26},{... | collective-permute-start | bytes 393224 | tf_op jit(solution)/shard_map/ppermute | solution.py:37
  (8 other events, 7.1 us)

commit v5 on v4

--- a/solution.py
+++ b/solution.py
@@ -227,13 +227,16 @@
         jnp.where(hit[None], coef.reshape(blocks, group, slots)[:, :, :, None], 0.0), axis=2
     ).reshape(1, blocks, group * blocks)
     me = lax.axis_index("col")
-    got = [part]
-    for ahead in range(1, group):
-        got.append(lax.ppermute(part, "col", [(i, (i + ahead) % group) for i in range(group)]))
+    got = part
+    while got.shape[0] < group:
+        ahead = got.shape[0]
+        more = got[: group - ahead]
+        ring = [(i, (i + ahead) % group) for i in range(group)]
+        got = jnp.concatenate([got, lax.ppermute(more, "col", ring)], axis=0)
     steps = jnp.arange(group, dtype=jnp.int32)
     mine = steps[:, None] == lax.rem(me - steps + group, group)[None, :]
     weights = jnp.sum(
-        jnp.where(mine[:, :, None, None], jnp.concatenate(got, axis=0)[None], 0.0), axis=1
+        jnp.where(mine[:, :, None, None], got[None], 0.0), axis=1
     ).reshape(group * blocks, group * blocks)
     high, low = spread(weights)
 

time: 261 us -> 261 us (level)
  starting transfers between devices: 52.8 us -> 46.7 us
  waiting for transfers between devices: 38.4 us -> 42.9 us
    ppermute x7 -> x3, waiting for transfers between devices: 6.78 us -> 11.9 us  [local(): got = jnp.concatenate([got, lax.ppermute(more, 'col', ring)], axis=0)]
    ppermute x7 -> x3, starting transfers between devices: 14 us -> 10.8 us  [local(): got = jnp.concatenate([got, lax.ppermute(more, 'col', ring)], axis=0)]
    all_to_all x2, starting transfers between devices: 11.7 us -> 8.86 us  [local(): lax.all_to_all(sums.reshape(strips.shape), 'col', split_axis=0, concat_ax...]
    unnamed x56 -> x49, local copies, waits for them, and re-layouts: 12.1 us -> 12.1 us
  transfers between devices with their start and end apart: 18 -> 14, of which waited for: 5 -> 6; matrix products, arithmetic and copies ran while one was open for 23% -> 23% of each run, Pallas kernels for 6% -> 6%
where the time goes in v5:
time: 261 us; the launch traced here: 259 us
  blocking collectives  53.3 us (20%)
  other arithmetic  53.1 us (20%)
  starting transfers between devices  46.7 us (18%)
  waiting for transfers between devices  42.9 us (16%)
  Pallas kernels  39.2 us (15%)
  local copies, waits for them, and re-layouts  15.5 us (6%)
  matrix products  5.96 us (2%)
    all_to_all x1, blocking collectives, local(): lax.all_to_all(strips, 'col', split_axis=0, concat_axis=0, tiled=True)  53.3 us
    all_to_all x2, waiting for transfers between devices, local(): lax.all_to_all(sums.reshape(strips.shape), 'col', split_axis=0, concat_ax...  29.5 us
    another operation x7, other arithmetic, local(): chol = jnp.linalg.cholesky(gram)  28.4 us
    another operation x6, other arithmetic, local(): jax.scipy.linalg.solve_triangular(chol, jnp.eye(bands, dtype=jnp.float32)...  21.3 us
    pallas_call x2, Pallas kernels, update(): pl.pallas_call(functools.partial(update_kernel, keep_dual), out_shape=sha...  16.5 us
    pallas_call x2, Pallas kernels, primal_step(): pl.pallas_call(primal_kernel, out_shape=jax.ShapeDtypeStruct((pixels, ato...  14.4 us
    ppermute x4, starting transfers between devices, beside(): lax.ppermute(last, axis, forward)  14.3 us
    unnamed x49, local copies, waits for them, and re-layouts  12.1 us
  transfers between devices with their start and end apart: 14, of which 6 were waited for; matrix products, arithmetic and copies ran while one was open for 23% of the time, Pallas kernels for 6%

profile of v5, /device:TPU:0, one launch (start us, length us, event | category | flops | bytes accessed | tf_op | source)
XLA Modules:
  0.0 259.2 jit_solution(12120015945708554628)
XLA Ops:
  0.6 2.3 copy.46
  2.9 1.7 copy.52
  4.7 7.4 %all-to-all-start = ((bf16[8,512,256]{2,1,0:T(8,128)(2,1)}), bf16[8,512,256]{2,1,0:T(8,128)(2,1)S(1)}, u32[]{:S(2)}, u32[]{:S(2)}) async-start(bf16[8,512,256]{2,1,0:T(8,128)(2,1)} %bitcast.82), calls=%async_computation | async-start | bytes 4194304 | tf_op jit(solution)/shard_map/all_to_all | solution.py:253
  12.9 2.0 collective-permute-start
  15.5 11.7 %cholesky.51 = f32[128,128]{1,0:T(8,128)S(1)} custom-call(f32[128,128]{1,0:T(8,128)S(1)} %cholesky.124), custom_call_target="Cholesky" | custom-call | tf_op jit(solution)/shard_map/jit(cholesky)/cholesky | solution.py:247
  27.2 9.8 %custom-call.15 = f32[1,128,128]{1,2,0:T(8,128)S(1)} custom-call(f32[1,128,128]{2,1,0:T(8,128)S(1)} %get-tuple-element.45), custom_call_target="InvertDiagBlocksLowerTriangular" | custom-call | tf_op jit(solution)/shard_map/jit(cholesky)/cholesky | solution.py:247
  37.4 5.5 %cholesky.110 = f32[60,60]{1,0:T(8,128)S(1)} custom-call(f32[60,60]{1,0:T(8,128)S(1)} %convolution_subtract_fusion.1), custom_call_target="Cholesky" | custom-call | tf_op jit(solution)/shard_map/jit(cholesky)/cholesky | solution.py:247
  46.3 4.8 %collective-permute-done = f32[1,4,32]{2,1,0:T(4,128)S(1)} collective-permute-done((f32[1,4,32]{2,1,0:T(4,128)S(1)}, f32[1,4,32]{2,1,0:T(4,128)S(1)}, u32[]{:S(2)}, u32[]{:S(2)}) %collective-permute-start) | collective-permute-done | bytes 544 | tf_op jit(solution)/shard_map/ppermute | solution.py:235
  51.1 5.5 %collective-permute-done.1 = f32[2,4,32]{2,1,0:T(4,128)S(1)} collective-permute-done((f32[2,4,32]{2,1,0:T(4,128)S(1)}, f32[2,4,32]{2,1,0:T(4,128)S(1)}, u32[]{:S(2)}, u32[]{:S(2)}) %collective-permute-start.1) | collective-permute-done | bytes 1056 | tf_op jit(solution)/shard_map/ppermute | solution.py:235
  56.6 8.8 %collective-permute-start.2 = (f32[4,4,32]{2,1,0:T(4,128)S(1)}, f32[4,4,32]{2,1,0:T(4,128)S(1)}, u32[]{:S(2)}, u32[]{:S(2)}) collective-permute-start(f32[4,4,32]{2,1,0:T(4,128)S(1)} %pad_maximum_fusion.2), channel_id=1, source_target_pairs={{0,4},{1,5},{2,6},{3,7},{4,0},{5,1},{6,2},{7,3},{8,12},{9,13},{10,... | collective-permute-start | bytes 6152 | tf_op jit(solution)/shard_map/ppermute | solution.py:235
  65.4 1.6 collective-permute-done.2
  69.9 3.8 %mix.2 = bf16[32,128,256]{2,1,0:T(8,128)(2,1)S(1)} custom-call(bf16[512,512]{1,0:T(8,128)(2,1)S(1)} %get-tuple-element.10.high_ref, bf16[512,512]{1,0:T(8,128)(2,1)S(1)} %copy-done.8, bf16[32,128,256]{2,1,0:T(8,128)(2,1)S(1)} %bitcast.73), custom_call_target="tpu_custom_call" | custom-call | tf_op jit(solution)/shard_map/mix/pallas_call | solution.py:83
  73.8 1.3 copy-done.2
  75.1 4.5 %all-to-all-start.1 = ((bf16[8,512,256]{2,1,0:T(8,128)(2,1)}), bf16[8,512,256]{2,1,0:T(8,128)(2,1)}, u32[]{:S(2)}, u32[]{:S(2)}) async-start(bf16[8,512,256]{2,1,0:T(8,128)(2,1)} %bitcast.74), calls=%async_computation.1 | async-start | bytes 4194304 | tf_op jit(solution)/shard_map/all_to_all | solution.py:263
  81.6 3.7 %collective-permute-start.3 = (bf16[32,2048]{1,0:T(8,128)(2,1)}, bf16[32,2048]{1,0:T(8,128)(2,1)}, u32[]{:S(2)}, u32[]{:S(2)}) collective-permute-start(bf16[32,2048]{1,0:T(8,128)(2,1)} %get-tuple-element.43), channel_id=1, source_target_pairs={{0,8},{8,16},{16,24},{1,9},{9,17},{17,25},{2,10},{10,18},{18,26},{... | collective-permute-start | bytes 393224 | tf_op jit(solution)/shard_map/ppermute | solution.py:37
  86.2 3.8 %collective-permute-start.5 = (bf16[16,2048]{1,0:T(8,128)(2,1)}, bf16[16,2048]{1,0:T(8,128)(2,1)S(1)}, u32[]{:S(2)}, u32[]{:S(2)}) collective-permute-start(bf16[16,2048]{1,0:T(8,128)(2,1)} %bitcast.68), channel_id=1, source_target_pairs={{0,1},{1,2},{2,3},{3,4},{4,5},{5,6},{6,7},{8,9},{9,10},{10,11},{11... | collective-permute-start | bytes 196616 | tf_op jit(solution)/shard_map/ppermute | solution.py:37
  90.6 1.5 collective-permute-start.6
  94.9 20.5 %custom-call.16 = f32[2,128,128]{1,2,0:T(8,128)S(1)} custom-call(f32[2,128,128]{2,1,0:T(8,128)} %pad_maximum_fusion), custom_call_target="InvertDiagBlocksLowerTriangular" | custom-call | tf_op jit(solution)/shard_map/jit(_solve_triangular)/triangular_solve | solution.py:256
  118.3 6.4 %primal.2.refs_0_ = f32[512,2048]{1,0:T(8,128)} custom-call(bf16[512,188]{1,0:T(8,128)(2,1)S(1)} %bitcast.77, bf16[188,2048]{1,0:T(8,128)(2,1)S(1)} %copy-done.1, f32[188,188]{1,0:T(8,128)S(1)} %fusion.inverse_ref, bf16[512,2048]{1,0:T(8,128)(2,1)S(1)} %bitcast.70), custom_call_target="tpu_custom_call" | custom-call | flops 1577058304 | bytes 12582912 | tf_op jit(solution)/shard_map/primal/pallas_call | solution.py:134
  124.8 2.1 all-to-all-done.1.refs_1_
  126.9 8.8 %update.2 = (bf16[512,2048]{1,0:T(8,128)(2,1)S(1)}, f32[512,2048]{1,0:T(8,128)}, bf16[8,512,256]{2,1,0:T(8,128)(2,1)S(1)}) custom-call(f32[512,2048]{1,0:T(8,128)} %primal.2.refs_0_, bf16[8,512,256]{2,1,0:T(8,128)(2,1)} %all-to-all-done.1.refs_1_, bf16[16,32,2048]{2,1,0:T(8,128)(2,1)} %refs_2_.1, bf16[32,2048]{1,0:T(8,128)(2,1)} %collective-permute-done.3.refs_3_, ...), custom_call_target="tpu_custom_call" | custom-call | tf_op jit(solution)/shard_map/update/pallas_call | solution.py:197
  135.7 53.3 %all_to_all.20 = bf16[8,512,256]{2,1,0:T(8,128)(2,1)S(1)} all-to-all(bf16[8,512,256]{2,1,0:T(8,128)(2,1)S(1)} %get-tuple-element.15), channel_id=1, replica_groups=mesh['row'=4,'col'=8] {'col'}, dimensions={0} | all-to-all | bytes 4194304 | tf_op jit(solution)/shard_map/all_to_all | solution.py:253
  189.0 3.8 %mix.3 = bf16[32,128,256]{2,1,0:T(8,128)(2,1)S(1)} custom-call(bf16[512,512]{1,0:T(8,128)(2,1)S(1)} %copy-done.6, bf16[512,512]{1,0:T(8,128)(2,1)S(1)} %copy-done.9, bf16[32,128,256]{2,1,0:T(8,128)(2,1)S(1)} %bitcast.76), custom_call_target="tpu_custom_call" | custom-call | tf_op jit(solution)/shard_map/mix/pallas_call | solution.py:83
  192.8 1.3 copy-done.3
  194.2 4.4 %all-to-all-start.3 = ((bf16[8,512,256]{2,1,0:T(8,128)(2,1)}), bf16[8,512,256]{2,1,0:T(8,128)(2,1)}, u32[]{:S(2)}, u32[]{:S(2)}) async-start(bf16[8,512,256]{2,1,0:T(8,128)(2,1)} %bitcast.75), calls=%async_computation.3 | async-start | bytes 4194304 | tf_op jit(solution)/shard_map/all_to_all | solution.py:263
  198.8 3.8 %collective-permute-start.9 = (bf16[16,2048]{1,0:T(8,128)(2,1)S(1)}, bf16[16,2048]{1,0:T(8,128)(2,1)S(1)}, u32[]{:S(2)}, u32[]{:S(2)}) collective-permute-start(bf16[16,2048]{1,0:T(8,128)(2,1)S(1)} %bitcast.87), channel_id=1, source_target_pairs={{0,1},{1,2},{2,3},{3,4},{4,5},{5,6},{6,7},{8,9},{9,10},{10,11},{11... | collective-permute-start | bytes 196616 | tf_op jit(solution)/shard_map/ppermute | solution.py:37
  205.3 3.0 %collective-permute-start.7 = (bf16[32,2048]{1,0:T(8,128)(2,1)S(1)}, bf16[32,2048]{1,0:T(8,128)(2,1)S(1)}, u32[]{:S(2)}, u32[]{:S(2)}) collective-permute-start(bf16[32,2048]{1,0:T(8,128)(2,1)S(1)} %get-tuple-element.39), channel_id=1, source_target_pairs={{0,8},{8,16},{16,24},{1,9},{9,17},{17,25},{2,10},{10,18},{18,26},{... | collective-permute-start | bytes 393224 | tf_op jit(solution)/shard_map/ppermute | solution.py:37
  208.3 8.0 %primal.3.refs_0_ = f32[512,2048]{1,0:T(8,128)} custom-call(bf16[512,188]{1,0:T(8,128)(2,1)S(1)} %bitcast.78, bf16[188,2048]{1,0:T(8,128)(2,1)S(1)} %copy-done.1, f32[188,188]{1,0:T(8,128)S(1)} %fusion.inverse_ref, bf16[512,2048]{1,0:T(8,128)(2,1)S(1)} %get-tuple-element.13.tile_ref, f32[512,2048]{1,0:T(8,128)} %get-tuple-element.14.rest_0_), custom_call_target="tpu_custom_call" | custom-call | flops 1577058304 | bytes 12582912 | tf_op jit(solution)/shard_map/primal/pallas_call | solution.py:134
  216.3 1.5 collective-permute-done.9.refs_5_
  219.1 27.5 %all-to-all-done.3.refs_1_ = bf16[8,512,256]{2,1,0:T(8,128)(2,1)} async-done(((bf16[8,512,256]{2,1,0:T(8,128)(2,1)}), bf16[8,512,256]{2,1,0:T(8,128)(2,1)}, u32[]{:S(2)}, u32[]{:S(2)}) %all-to-all-start.3) | async-done | bytes 2097184 | tf_op jit(solution)/shard_map/all_to_all | solution.py:263
  248.3 7.7 %update.3 = bf16[512,2048]{1,0:T(8,128)(2,1)} custom-call(f32[512,2048]{1,0:T(8,128)} %primal.3.refs_0_, bf16[8,512,256]{2,1,0:T(8,128)(2,1)} %all-to-all-done.3.refs_1_, bf16[16,32,2048]{2,1,0:T(8,128)(2,1)S(1)} %bitcast.72, bf16[32,2048]{1,0:T(8,128)(2,1)S(1)} %copy-done.11, bf16[32,2048]{1,0:T(8,128)(2,1)S(1)} %collective-permute-done.8.refs_4_, ...), custom_call_target="tpu_custom_call" | custom-call | tf_op jit(solution)/shard_map/update/pallas_call | solution.py:197
  256.0 2.3 fusion.25
  (105 shorter events, 22.7 us)
Async XLA Ops:
  4.6 7.4 %copy-start.17 = (f32[4,1,8]{2,1,0:T(1,128)S(1)}, f32[4,1,8]{2,1,0:T(1,128)}, u32[]{:S(2)}) copy-start(f32[4,1,8]{2,1,0:T(1,128)} %param.15) | copy-start | bytes 388
  4.6 7.4 %copy-start.20 = (s32[4,1]{0,1:T(1,128)S(1)}, s32[4,1]{0,1:T(1,128)}, u32[]{:S(2)}) copy-start(s32[4,1]{0,1:T(1,128)} %param.14) | copy-start | bytes 52
  4.6 7.7 %copy-start.18 = (s32[4,1,8]{2,1,0:T(1,128)S(1)}, s32[4,1,8]{2,1,0:T(1,128)}, u32[]{:S(2)}) copy-start(s32[4,1,8]{2,1,0:T(1,128)} %param.13) | copy-start | bytes 388
  4.6 7.7 %copy-start.19 = (s32[4,1,8]{2,1,0:T(1,128)S(1)}, s32[4,1,8]{2,1,0:T(1,128)}, u32[]{:S(2)}) copy-start(s32[4,1,8]{2,1,0:T(1,128)} %param.12) | copy-start | bytes 388
  4.7 8.0 %copy-start.21 = (s32[1,8,2]{1,2,0:T(2,128)S(1)}, s32[1,8,2]{1,2,0:T(2,128)}, u32[]{:S(2)}) copy-start(s32[1,8,2]{1,2,0:T(2,128)} %param.16) | copy-start | bytes 196
  4.7 10.2 %copy-start.1 = (bf16[188,2048]{1,0:T(8,128)(2,1)S(1)}, bf16[188,2048]{1,0:T(8,128)(2,1)}, u32[]{:S(2)}) copy-start(bf16[188,2048]{1,0:T(8,128)(2,1)} %library_ref.3) | copy-start | bytes 2310148
  4.7 64.0 %all-to-all-start = ((bf16[8,512,256]{2,1,0:T(8,128)(2,1)}), bf16[8,512,256]{2,1,0:T(8,128)(2,1)S(1)}, u32[]{:S(2)}, u32[]{:S(2)}) async-start(bf16[8,512,256]{2,1,0:T(8,128)(2,1)} %bitcast.82), calls=%async_computation | async-start | bytes 4194304 | tf_op jit(solution)/shard_map/all_to_all | solution.py:253
  12.9 38.2 %collective-permute-start = (f32[1,4,32]{2,1,0:T(4,128)S(1)}, f32[1,4,32]{2,1,0:T(4,128)S(1)}, u32[]{:S(2)}, u32[]{:S(2)}) collective-permute-start(f32[1,4,32]{2,1,0:T(4,128)S(1)} %reshape.170), channel_id=1, source_target_pairs={{0,1},{1,2},{2,3},{3,4},{4,5},{5,6},{6,7},{7,0},{8,9},{9,10},{10,1... | collective-permute-start | bytes 1544 | tf_op jit(solution)/shard_map/ppermute | solution.py:235
  51.1 5.5 %collective-permute-start.1 = (f32[2,4,32]{2,1,0:T(4,128)S(1)}, f32[2,4,32]{2,1,0:T(4,128)S(1)}, u32[]{:S(2)}, u32[]{:S(2)}) collective-permute-start(f32[2,4,32]{2,1,0:T(4,128)S(1)} %pad_maximum_fusion.3), channel_id=1, source_target_pairs={{0,2},{1,3},{2,4},{3,5},{4,6},{5,7},{6,0},{7,1},{8,10},{9,11},{10,... | collective-permute-start | bytes 3080 | tf_op jit(solution)/shard_map/ppermute | solution.py:235
  56.6 10.4 %collective-permute-start.2 = (f32[4,4,32]{2,1,0:T(4,128)S(1)}, f32[4,4,32]{2,1,0:T(4,128)S(1)}, u32[]{:S(2)}, u32[]{:S(2)}) collective-permute-start(f32[4,4,32]{2,1,0:T(4,128)S(1)} %pad_maximum_fusion.2), channel_id=1, source_target_pairs={{0,4},{1,5},{2,6},{3,7},{4,0},{5,1},{6,2},{7,3},{8,12},{9,13},{10,... | collective-permute-start | bytes 6152 | tf_op jit(solution)/shard_map/ppermute | solution.py:235
  68.7 5.1 %copy-start.5 = (bf16[512,512]{1,0:T(8,128)(2,1)}, bf16[512,512]{1,0:T(8,128)(2,1)S(1)}, u32[]{:S(2)}) copy-start(bf16[512,512]{1,0:T(8,128)(2,1)S(1)} %get-tuple-element.10.high_ref) | copy-start | bytes 1572868
  68.7 1.2 copy-start.8
  73.8 1.3 copy-start.2
  75.1 4.5 %copy-start = (bf16[16,32,2048]{2,1,0:T(8,128)(2,1)S(1)}, bf16[16,32,2048]{2,1,0:T(8,128)(2,1)}, u32[]{:S(2)}) copy-start(bf16[16,32,2048]{2,1,0:T(8,128)(2,1)} %refs_2_.1) | copy-start | bytes 6291460
  75.1 18.4 %copy-start.15 = (f32[188,188]{1,0:T(8,128)S(1)}, f32[188,188]{1,0:T(8,128)}, u32[]{:S(2)}) copy-start(f32[188,188]{1,0:T(8,128)} %select_select_fusion) | copy-start | bytes 424132
  75.1 51.8 %all-to-all-start.1 = ((bf16[8,512,256]{2,1,0:T(8,128)(2,1)}), bf16[8,512,256]{2,1,0:T(8,128)(2,1)}, u32[]{:S(2)}, u32[]{:S(2)}) async-start(bf16[8,512,256]{2,1,0:T(8,128)(2,1)} %bitcast.74), calls=%async_computation.1 | async-start | bytes 4194304 | tf_op jit(solution)/shard_map/all_to_all | solution.py:263
  79.6 38.7 %copy-start.4 = (bf16[16,32,188]{2,1,0:T(8,128)(2,1)S(1)}, bf16[16,32,188]{2,1,0:T(8,128)(2,1)}, u32[]{:S(2)}) copy-start(bf16[16,32,188]{2,1,0:T(8,128)(2,1)} %param.9) | copy-start | bytes 577540
  80.4 44.4 %collective-permute-start.4 = (bf16[32,2048]{1,0:T(8,128)(2,1)}, bf16[32,2048]{1,0:T(8,128)(2,1)S(1)}, u32[]{:S(2)}, u32[]{:S(2)}) collective-permute-start(bf16[32,2048]{1,0:T(8,128)(2,1)} %get-tuple-element.42), channel_id=1, source_target_pairs={{8,0},{16,8},{24,16},{9,1},{17,9},{25,17},{10,2},{18,10},{26,18},{... | collective-permute-start | bytes 393224 | tf_op jit(solution)/shard_map/ppermute | solution.py:37
  81.6 43.1 %collective-permute-start.3 = (bf16[32,2048]{1,0:T(8,128)(2,1)}, bf16[32,2048]{1,0:T(8,128)(2,1)}, u32[]{:S(2)}, u32[]{:S(2)}) collective-permute-start(bf16[32,2048]{1,0:T(8,128)(2,1)} %get-tuple-element.43), channel_id=1, source_target_pairs={{0,8},{8,16},{16,24},{1,9},{9,17},{17,25},{2,10},{10,18},{18,26},{... | collective-permute-start | bytes 393224 | tf_op jit(solution)/shard_map/ppermute | solution.py:37
  86.2 38.6 %collective-permute-start.5 = (bf16[16,2048]{1,0:T(8,128)(2,1)}, bf16[16,2048]{1,0:T(8,128)(2,1)S(1)}, u32[]{:S(2)}, u32[]{:S(2)}) collective-permute-start(bf16[16,2048]{1,0:T(8,128)(2,1)} %bitcast.68), channel_id=1, source_target_pairs={{0,1},{1,2},{2,3},{3,4},{4,5},{5,6},{6,7},{8,9},{9,10},{10,11},{11... | collective-permute-start | bytes 196616 | tf_op jit(solution)/shard_map/ppermute | solution.py:37
  90.6 34.1 %collective-permute-start.6 = (bf16[16,2048]{1,0:T(8,128)(2,1)}, bf16[16,2048]{1,0:T(8,128)(2,1)}, u32[]{:S(2)}, u32[]{:S(2)}) collective-permute-start(bf16[16,2048]{1,0:T(8,128)(2,1)} %bitcast.67), channel_id=1, source_target_pairs={{1,0},{2,1},{3,2},{4,3},{5,4},{6,5},{7,6},{9,8},{10,9},{11,10},{12... | collective-permute-start | bytes 196616 | tf_op jit(solution)/shard_map/ppermute | solution.py:37
  118.3 8.6 %copy-start.14 = (f32[2048]{0:T(1024)S(1)}, f32[2048]{0:T(1024)}, u32[]{:S(2)}) copy-start(f32[2048]{0:T(1024)} %param.17) | copy-start | bytes 24580
  135.7 53.3 %copy-start.6 = (bf16[512,512]{1,0:T(8,128)(2,1)S(1)}, bf16[512,512]{1,0:T(8,128)(2,1)}, u32[]{:S(2)}) copy-start(bf16[512,512]{1,0:T(8,128)(2,1)} %copy-done.5) | copy-start | bytes 1572868
  135.7 53.3 %copy-start.9 = (bf16[512,512]{1,0:T(8,128)(2,1)S(1)}, bf16[512,512]{1,0:T(8,128)(2,1)}, u32[]{:S(2)}) copy-start(bf16[512,512]{1,0:T(8,128)(2,1)} %copy-done.7) | copy-start | bytes 1572868
  192.8 1.3 copy-start.3
  194.2 52.4 %all-to-all-start.3 = ((bf16[8,512,256]{2,1,0:T(8,128)(2,1)}), bf16[8,512,256]{2,1,0:T(8,128)(2,1)}, u32[]{:S(2)}, u32[]{:S(2)}) async-start(bf16[8,512,256]{2,1,0:T(8,128)(2,1)} %bitcast.75), calls=%async_computation.3 | async-start | bytes 4194304 | tf_op jit(solution)/shard_map/all_to_all | solution.py:263
  198.8 19.0 %collective-permute-start.9 = (bf16[16,2048]{1,0:T(8,128)(2,1)S(1)}, bf16[16,2048]{1,0:T(8,128)(2,1)S(1)}, u32[]{:S(2)}, u32[]{:S(2)}) collective-permute-start(bf16[16,2048]{1,0:T(8,128)(2,1)S(1)} %bitcast.87), channel_id=1, source_target_pairs={{0,1},{1,2},{2,3},{3,4},{4,5},{5,6},{6,7},{8,9},{9,10},{10,11},{11... | collective-permute-start | bytes 196616 | tf_op jit(solution)/shard_map/ppermute | solution.py:37
  202.6 15.2 %collective-permute-start.10 = (bf16[16,2048]{1,0:T(8,128)(2,1)S(1)}, bf16[16,2048]{1,0:T(8,128)(2,1)S(1)}, u32[]{:S(2)}, u32[]{:S(2)}) collective-permute-start(bf16[16,2048]{1,0:T(8,128)(2,1)S(1)} %bitcast.86), channel_id=1, source_target_pairs={{1,0},{2,1},{3,2},{4,3},{5,4},{6,5},{7,6},{9,8},{10,9},{11,10},{12... | collective-permute-start | bytes 196616 | tf_op jit(solution)/shard_map/ppermute | solution.py:37
  204.0 14.5 %collective-permute-start.8 = (bf16[32,2048]{1,0:T(8,128)(2,1)S(1)}, bf16[32,2048]{1,0:T(8,128)(2,1)S(1)}, u32[]{:S(2)}, u32[]{:S(2)}) collective-permute-start(bf16[32,2048]{1,0:T(8,128)(2,1)S(1)} %get-tuple-element.38), channel_id=1, source_target_pairs={{8,0},{16,8},{24,16},{9,1},{17,9},{25,17},{10,2},{18,10},{26,18},{... | collective-permute-start | bytes 393224 | tf_op jit(solution)/shard_map/ppermute | solution.py:37
  205.3 13.2 %collective-permute-start.7 = (bf16[32,2048]{1,0:T(8,128)(2,1)S(1)}, bf16[32,2048]{1,0:T(8,128)(2,1)S(1)}, u32[]{:S(2)}, u32[]{:S(2)}) collective-permute-start(bf16[32,2048]{1,0:T(8,128)(2,1)S(1)} %get-tuple-element.39), channel_id=1, source_target_pairs={{0,8},{8,16},{16,24},{1,9},{9,17},{17,25},{2,10},{10,18},{18,26},{... | collective-permute-start | bytes 393224 | tf_op jit(solution)/shard_map/ppermute | solution.py:37
  246.5 0.9 copy-start.11
  247.4 0.8 copy-start.13
  (4 other events, 2.7 us)
